TPU v7x, 32 devices: a whole 2x2x4 slice. The times are simulated.
32 devices in a mesh: bx: 4 (over z), by: 8 (over y, x, core).
Axes of the slice: x: 2, y: 2, z: 4, core: 2. Of those that a mesh axis runs over, the one named last changes fastest.
Arguments:
- positions: float32 [3, 4096], P(None, ('bx', 'by')), may hold values from 0 to 8, as said below
- tangent: float32 [3, 4096], P(None, ('bx', 'by')), may hold values from -6 to 6
- embedding: float32 [4096, 256], P(('bx', 'by')), may hold values from -6 to 6
- counts: int32 [32], P(('bx', 'by')), may hold values from 64 to 128, as said below
- neighbours: int32 [32, 4096], P(None, ('bx', 'by')), may hold values from 0 to 191, as said below
- send_rows: int32 [32, 64], P(('bx', 'by')), may hold values from 0 to 127
- w_one_in: float32 [256, 256], replicated, may hold values from -0.375 to 0.375
- w_one_out: float32 [256, 512], replicated, may hold values from -0.375 to 0.375
- filter_one: float32 [20, 512], replicated, may hold values from -0.3125 to 0.3125
- w_left: float32 [256, 256], replicated, may hold values from -0.375 to 0.375
- w_right: float32 [256, 256], replicated, may hold values from -0.375 to 0.375
- w_two_in: float32 [256, 256], replicated, may hold values from -0.375 to 0.375
- w_two_out: float32 [256, 256], replicated, may hold values from -0.375 to 0.375
- filter_two: float32 [20, 256], replicated, may hold values from -0.3125 to 0.3125
- w_hidden: float32 [256, 256], replicated, may hold values from -0.375 to 0.375
- w_energy: float32 [256], replicated, may hold values from -0.375 to 0.375
Outputs:
- forces: float32 [3, 4096], P(None, ('bx', 'by'))
- hessian_tangent: float32 [3, 4096], P(None, ('bx', 'by'))
Inputs may be any that keep to these rules, and one draw needn't show every extreme that they name: The live atoms of a brick are its first counts rows; every count is a multiple of 32; some brick holds 128 live atoms and some 128 // 2. `neighbours`: the 32 slots of an atom are distinct; each is a live row of its own brick other than the atom's own row, or a slot of a neighbouring brick that exists in the sheet. `positions`: atom n lies within one unit of its brick's indices along x and y, with the third coordinate in [0, 0.3).
All inputs are finite; a program needn't handle non-finite values.
Results may differ from a plain program's by a relative error of at most 0.0003.
Values sent between devices are 32-bit elements; how exact they have to be, the bound alone decides.
No kernel may reach another device: no remote copies, remote signals or barrier semaphores. Data moves between devices by JAX's collectives and lax.ppermute only.
A program may use at most 192 MiB of HBM per device.

v0:
```python
import functools
import math

import jax
import jax.numpy as jnp
from jax import lax
from jax.experimental import pallas as pl
from jax.experimental.pallas import tpu as pltpu
from jax.sharding import PartitionSpec as P

f32 = jnp.float32
bf16 = jnp.bfloat16
cutoff_radius = 3.0
softening = 0.01
wave = math.pi / cutoff_radius
offsets = ((-1, -1), (-1, 0), (-1, 1), (0, -1), (0, 1), (1, -1), (1, 0), (1, 1))
lanes = 128
wide = 256
row_block = 32
nn_dims = (((1,), (0,)), ((), ()))
nt_dims = (((1,), (1,)), ((), ()))

U, UD, DD, RI = 0, 3, 6, 7
geo_slots = 8
P0, P1, P2, SN, CS, RS, RC = 0, 1, 2, 3, 4, 5, 6
osc_slots = 7
own_group = 2
ghost_group = 5


def split(value):
    high = value.astype(bf16)
    return high, (value - high.astype(f32)).astype(bf16)


def mxu(left, right, dims=nn_dims):
    return lax.dot_general(left, right, dims, preferred_element_type=f32)


def three(lh, ll, rh, rl, dims=nn_dims):
    return mxu(lh, rh, dims) + mxu(ll, rh, dims) + mxu(lh, rl, dims)


def dot3(left, right, dims=nn_dims):
    return three(*split(left), *split(right[...]), dims)


def sigmoid(value):
    return 1.0 / (1.0 + jnp.exp(-jnp.maximum(value, -80.0)))


def silu_parts(value):
    gate = sigmoid(value)
    first = gate * (1.0 + value * (1.0 - gate))
    second = gate * (1.0 - gate) * (2.0 + value * (1.0 - 2.0 * gate))
    return value * gate, first, second


def sin_cos(theta):
    t = jnp.minimum(theta, 6.0) * 0.25
    x = t * t
    s = -1.0 / 39916800.0 + x * (1.0 / 6227020800.0)
    s = 1.0 / 362880.0 + x * s
    s = -1.0 / 5040.0 + x * s
    s = 1.0 / 120.0 + x * s
    s = -1.0 / 6.0 + x * s
    s = t + t * x * s
    c = 1.0 / 479001600.0 - x * (1.0 / 87178291200.0)
    c = -1.0 / 3628800.0 + x * c
    c = 1.0 / 40320.0 + x * c
    c = -1.0 / 720.0 + x * c
    c = 1.0 / 24.0 + x * c
    c = -0.5 + x * c
    c = 1.0 + x * c
    s, c = 2.0 * s * c, 1.0 - 2.0 * s * s
    return 2.0 * s * c, 1.0 - 2.0 * s * s


def fill_geometry(geo, osc, first, second, mask_at, height, members):
    repeats = wide // members
    group = lax.broadcasted_iota(jnp.int32, (1, wide), 1) // members
    for start in range(0, height, row_block):
        rows = pl.ds(start, row_block)
        off = [first(i, start) - second(i, start) for i in range(3)]
        move = [first(i + 3, start) - second(i + 3, start) for i in range(3)]
        square = off[0] * off[0] + off[1] * off[1] + off[2] * off[2] + softening
        inverse = lax.rsqrt(square)
        inverse = inverse * (1.5 - 0.5 * square * inverse * inverse)
        theta = wave * (square * inverse)
        unit = [o * inverse for o in off]
        speed = unit[0] * move[0] + unit[1] * move[1] + unit[2] * move[2]
        for i in range(3):
            geo[U + i, rows, :] = unit[i]
            geo[UD + i, rows, :] = (move[i] - unit[i] * speed) * inverse
        sn, cs = sin_cos(theta)
        g0 = (0.5 * cs + 0.5) * inverse
        g1 = ((-0.5 * wave) * sn - g0) * inverse
        g2 = ((-0.5 * wave * wave) * cs - 2.0 * g1) * inverse
        mask = mask_at(start)
        geo[DD, rows, :] = speed
        osc[P0, rows, :] = mask * g0
        osc[P1, rows, :] = mask * g1
        osc[P2, rows, :] = mask * g2
        geo[RI, rows, :] = inverse
        turn_s, turn_c = sn, cs
        state_s, state_c = sn, cs
        for i in range(1, repeats):
            turn_s, turn_c = turn_s * cs + turn_c * sn, turn_c * cs - turn_s * sn
            state_s = jnp.where(group >= i, turn_s, state_s)
            state_c = jnp.where(group >= i, turn_c, state_c)
        osc[SN, rows, :] = state_s
        osc[CS, rows, :] = state_c
        osc[RS, rows, :] = turn_s
        osc[RC, rows, :] = turn_c


def order_factor(step, members):
    repeats = wide // members
    group = lax.broadcasted_iota(jnp.int32, (1, wide), 1) // members
    return (group + (step * repeats + 1)).astype(f32) * wave


def rotate(wave_state, osc, rows, s, c):
    rs = osc[RS, rows, :]
    rc = osc[RC, rows, :]
    wave_state[0, rows, :] = s * rc + c * rs
    wave_state[1, rows, :] = c * rc - s * rs


def steps(count, members, body):
    group = own_group if members == lanes else ghost_group
    if group >= count:
        for step in range(count):
            body(step, step % 2)
        return

    def several(index, carry):
        for place in range(group):
            body(index * group + place, place % 2)
        return carry

    lax.fori_loop(0, count // group, several, 0)


def start_state(state, osc, height):
    state[0, 0:height, :] = osc[SN, 0:height, :]
    state[1, 0:height, :] = osc[CS, 0:height, :]


def listed(nbr_ref, start, members):
    slot = lax.broadcasted_iota(jnp.int32, (members, lanes), 0) + start
    found = nbr_ref[0:1, :] == slot
    for k in range(1, nbr_ref.shape[0]):
        found = found | (nbr_ref[k : k + 1, :] == slot)
    return jnp.where(found, 1.0, 0.0).astype(f32)


def geometry_by_atom(geo, osc, columns, table, mask, wbox):
    members = mask.shape[0]
    repeats = wide // members
    table = jnp.concatenate([table] * repeats, 1)
    wbox[...] = jnp.concatenate([mask] * repeats, 0).T
    fill_geometry(
        geo,
        osc,
        lambda i, start: table[i : i + 1, :],
        lambda i, start: columns[start : start + row_block, i : i + 1],
        lambda start: wbox[start : start + row_block, :],
        geo.shape[1],
        members,
    )


def geometry_by_slot(geo, osc, columns, centre, mask, wbox):
    height, own_rows = mask.shape
    repeats = wide // own_rows
    centre = jnp.concatenate([centre] * repeats, 1)
    wbox[0:height, :] = jnp.concatenate([mask] * repeats, 1)
    fill_geometry(
        geo,
        osc,
        lambda i, start: columns[start : start + row_block, i : i + 1],
        lambda i, start: centre[i : i + 1, :],
        lambda start: wbox[start : start + row_block, :],
        height,
        own_rows,
    )


def scaled_rows(pair, slot, step, filter_ref, columns, value):
    members = value.shape[0]
    for i in range(wide // members):
        row = filter_ref[pl.ds(step * (wide // members) + i, 1), columns]
        h, l = split(row * value)
        pair[0][slot, i * members : (i + 1) * members, :] = h
        pair[1][slot, i * members : (i + 1) * members, :] = l


def put_split(pair, start, value):
    h, l = split(value)
    pair[0][start : start + value.shape[0], :] = h
    pair[1][start : start + value.shape[0], :] = l


def at(pair, index):
    return pair[0].at[index], pair[1].at[index]


def basis_rows(kept, state, geo, osc, step, factor, start, height):
    rows = pl.ds(start, row_block)
    s, c = state[0, rows, :], state[1, rows, :]
    p0 = osc[P0, rows, :]
    b = p0 * s
    bd = (osc[P1, rows, :] * s + factor * (p0 * c)) * geo[DD, rows, :]
    put_split(kept, start, b)
    put_split(kept, height + start, bd)
    rotate(state, osc, rows, s, c)
    return b, bd


def first_messages(acc, geo, osc, state, work, scalars, vectors, phi, filt, members, chunks):
    height = geo.shape[1]
    channels = phi.shape[1] // 2
    top = 2 * height
    start_state(state, osc, height)

    def chunk(step, slot):
        factor = order_factor(step, members)
        scaled_rows(scalars, slot, step, filt, slice(0, channels), phi[:, :channels])
        scaled_rows(vectors, slot, step, filt, slice(channels, 2 * channels), phi[:, channels:])
        now = at(work, slot)
        for start in range(0, height, row_block):
            rows = pl.ds(start, row_block)
            b, bd = basis_rows(now, state, geo, osc, step, factor, start, height)
            for i in range(3):
                unit = geo[U + i, rows, :]
                put_split(now, (2 + i) * height + start, unit * b)
                put_split(
                    now, (5 + i) * height + start, geo[UD + i, rows, :] * b + unit * bd
                )
        ah, al = now
        acc[:top, :] += three(ah[:top, :], al[:top, :], scalars[0][slot], scalars[1][slot])
        acc[top:, :] += three(ah[top:, :], al[top:, :], vectors[0][slot], vectors[1][slot])

    steps(chunks, members, chunk)


def second_messages(acc, basis_at, plain, dotted, filt, value, chunks):
    height = acc.shape[0] // 2
    channels = acc.shape[1]

    def chunk(step, slot):
        scaled_rows(plain, slot, step, filt, slice(None), value[:, :channels])
        scaled_rows(dotted, slot, step, filt, slice(None), value[:, channels:])
        ah, al = basis_at(step, slot)
        acc[...] += three(ah[...], al[...], plain[0][slot], plain[1][slot])
        acc[height:, :] += three(
            ah[:height, :], al[:height, :], dotted[0][slot], dotted[1][slot]
        )

    steps(chunks, value.shape[0], chunk)


def plain_basis(kept, geo, osc, state, members, step, height):
    factor = order_factor(step, members)
    for start in range(0, height, row_block):
        basis_rows(kept, state, geo, osc, step, factor, start, height)


def full_basis(kept, geo, osc, state, members, step):
    height = geo.shape[1]
    factor = order_factor(step, members)
    for start in range(0, height, row_block):
        rows = pl.ds(start, row_block)
        s, c = state[0, rows, :], state[1, rows, :]
        p0, p1 = osc[P0, rows, :], osc[P1, rows, :]
        b = p0 * s
        kept[0, rows, :] = b
        kept[1, rows, :] = p1 * s + factor * (p0 * c)
        kept[2, rows, :] = (
            osc[P2, rows, :] * s + factor * (2.0 * p1 * c - factor * b)
        ) * geo[DD, rows, :]
        rotate(state, osc, rows, s, c)


def table_cotangents(back, basis_at, plain, dotted, filt, cot, chunks):
    channels = filt.shape[1]
    own_rows = cot.shape[0] // 2
    height = back.shape[0]
    back[...] = jnp.zeros_like(back)

    def chunk(step, slot):
        scaled_rows(plain, slot, step, filt, slice(None), cot[0:own_rows, :])
        scaled_rows(dotted, slot, step, filt, slice(None), cot[own_rows:, :])
        ah, al = basis_at(step, slot)
        both = three(ah[...], al[...], plain[0][slot], plain[1][slot])
        back[:, :channels] += both[:height]
        back[:, channels:] += both[height:] + three(
            ah[:height, :], al[:height, :], dotted[0][slot], dotted[1][slot]
        )

    steps(chunks, own_rows, chunk)


def folded(value, members):
    total = value[:, :lanes] + value[:, lanes:]
    if members < lanes:
        total = total + pltpu.roll(total, members, 1)
    return total


def second_pairs(pair, result, split_cot, basis_at, plain, dotted, filt, value, chunks):
    height = pair.shape[1]
    channels = filt.shape[1]
    pair[...] = jnp.zeros_like(pair)
    ah, al = split_cot

    def chunk(step, slot):
        scaled_rows(plain, slot, step, filt, slice(None), value[:, :channels])
        scaled_rows(dotted, slot, step, filt, slice(None), value[:, channels:])
        both = three(ah[...], al[...], plain[0][slot], plain[1][slot], nt_dims)
        dot = both[height:] + three(
            ah[:height, :], al[:height, :], dotted[0][slot], dotted[1][slot], nt_dims
        )
        basis = basis_at(step, slot)
        for start in range(0, height, row_block):
            rows = pl.ds(start, row_block)
            b1 = basis[1, rows, :]
            g = both[start : start + row_block]
            pair[0, rows, :] += b1 * g
            pair[1, rows, :] += basis[2, rows, :] * g + b1 * dot[start : start + row_block]

    members = value.shape[0]
    steps(chunks, members, chunk)
    result[0] = folded(pair[0], members)
    result[1] = folded(pair[1], members)


def first_pairs(pair, spaces, split_cot, geo, basis_at, factors_at, members, chunks):
    height = geo.shape[1]
    pair[...] = jnp.zeros_like(pair)
    ch, cl = split_cot
    top = 2 * height

    def chunk(step, slot):
        cots = spaces.at[slot]
        scalars, vectors = factors_at(step, slot)
        cots[:top, :] = three(
            ch[:top, :], cl[:top, :], scalars[0][...], scalars[1][...], nt_dims
        )
        cots[top:, :] = three(
            ch[top:, :], cl[top:, :], vectors[0][...], vectors[1][...], nt_dims
        )
        basis = basis_at(step, slot)
        for start in range(0, height, row_block):
            rows = pl.ds(start, row_block)
            b, b1, b2d = [basis[i, rows, :] for i in range(3)]
            b1d = b1 * geo[DD, rows, :]
            along = cots[start : start + row_block, :]
            along_dot = cots[height + start : height + start + row_block, :]
            for i in range(3):
                place = (2 + i) * height + start
                g = cots[place : place + row_block, :]
                place = (5 + i) * height + start
                gd = cots[place : place + row_block, :]
                unit = geo[U + i, rows, :]
                along = along + unit * g
                along_dot = along_dot + unit * gd + geo[UD + i, rows, :] * g
                pair[2 + i, rows, :] += b * g
                pair[5 + i, rows, :] += b * gd + b1d * g
            pair[0, rows, :] += b1 * along
            pair[1, rows, :] += b2d * along + b1 * along_dot

    steps(chunks, members, chunk)


def neighbour_id(target, sizes):
    along = lax.axis_index("bx") + target[0]
    across = lax.axis_index("by") + target[1]
    inside = (along >= 0) & (along < sizes[0]) & (across >= 0) & (across < sizes[1])
    device = jnp.clip(along, 0, sizes[0] - 1) * sizes[1] + jnp.clip(across, 0, sizes[1] - 1)
    return device, inside


def send_chunks(r, chunk_at, sizes):
    for number, target in enumerate(offsets):
        device, inside = neighbour_id(target, sizes)
        copy = pltpu.make_async_copy(chunk_at(number), r.out.at[device], r.moves.at[number])

        @pl.when(inside)
        def _():
            copy.start()

    for number, target in enumerate(offsets):
        device, inside = neighbour_id(target, sizes)
        copy = pltpu.make_async_copy(chunk_at(number), r.out.at[device], r.moves.at[number])

        @pl.when(inside)
        def _():
            copy.wait()


def send_groups(r, table, sizes):
    count = r.out.shape[1]
    send_chunks(r, lambda number: table.at[number * count : (number + 1) * count, :], sizes)


def send_gathered(r, table, stage, send_ref, sizes):
    for slot in range(stage.shape[0]):
        stage[slot : slot + 1, :] = table[pl.ds(send_ref[0, slot], 1), :]
    send_groups(r, stage, sizes)


def receive(r, table, sizes):
    count = r.arrived.shape[1]

    def each(act):
        for number, target in enumerate(offsets):
            device, inside = neighbour_id(target, sizes)
            copy = pltpu.make_async_copy(
                r.arrived.at[device],
                table.at[number * count : (number + 1) * count, :],
                r.moves.at[number],
            )

            @pl.when(inside)
            def _():
                act(copy)

    each(lambda copy: copy.start())
    return lambda: each(lambda copy: copy.wait())


def add_returned(total, table, send_ref, sizes):
    count = table.shape[0] // 8
    for number, target in enumerate(offsets):
        device, inside = neighbour_id(target, sizes)

        @pl.when(inside)
        def _():
            for slot in range(number * count, (number + 1) * count):
                total[pl.ds(send_ref[0, slot], 1), :] += table[slot : slot + 1, :]


def offset_gradients(geo, pair, second, members, by_slot, by_atom):
    near = [folded(pair[i], members) for i in range(8)]
    height = geo.shape[1]
    units = [geo[U + i, :, :lanes] for i in range(3)]
    moves = [geo[UD + i, :, :lanes] for i in range(3)]
    inverse = geo[RI, :, :lanes]
    speed = geo[DD, :, :lanes]
    along = near[0] + second[0]
    along_dot = near[1] + second[1]
    turn, turn_dot = near[2:5], near[5:8]
    inner = units[0] * turn[0] + units[1] * turn[1] + units[2] * turn[2]
    inner_dot = sum(units[i] * turn_dot[i] + moves[i] * turn[i] for i in range(3))
    rate = speed * inverse
    lane = lax.broadcasted_iota(jnp.int32, (1, lanes), 1)
    sums = jnp.zeros((height, lanes), f32)
    for i in range(3):
        part = (turn[i] - units[i] * inner) * inverse
        grad = along * units[i] + part
        grad_dot = (
            along_dot * units[i]
            + along * moves[i]
            + (turn_dot[i] - moves[i] * inner - units[i] * inner_dot) * inverse
            - rate * part
        )
        for row, value in ((i, grad), (3 + i, grad_dot)):
            by_slot[row : row + 1, :] = jnp.sum(value, 0, keepdims=True)
            if members < lanes:
                value = jnp.where(lane < members, value, 0.0)
            sums = jnp.where(lane == row, -jnp.sum(value, 1, keepdims=True), sums)
    by_atom[...] = sums


def pack_kernel(sizes, r):
    channels = r.embedding.shape[1]
    r.box[...] = jnp.zeros_like(r.box)
    r.need(r.positions, r.tangent)
    r.box[0:3, :] = r.positions[...]
    r.box[3:6, :] = r.tangent[...]
    r.table[:, channels:] = r.box[...].T
    r.need(r.embedding)
    r.table[:, :channels] = r.embedding[...]
    r.need(r.send_rows)
    send_gathered(r, r.table, r.stage, r.send_rows, sizes)


def first_own_kernel(scale, chunks, r):
    own_rows = r.positions.shape[1]
    r.box[...] = jnp.zeros_like(r.box)
    r.need(r.positions, r.tangent, r.neighbours)
    r.box[0:3, :] = r.positions[...]
    r.box[3:6, :] = r.tangent[...]
    r.cols[...] = r.box[...].T
    r.mask_own[...] = listed(r.neighbours, 0, own_rows)
    r.mask_ghost[...] = listed(r.neighbours, own_rows, r.mask_ghost.shape[0])
    r.put(r.box, r.cols, r.mask_own, r.mask_ghost)
    geometry_by_atom(r.geo_own, r.osc_own, r.cols[...], r.box[...], r.mask_own[...], r.wbox)
    r.put(r.geo_own, r.osc_own)
    r.need(r.w_one_in, r.w_one_out, r.embedding, r.filter_one, r.filter_two)
    r.filt_one[...] = r.filter_one[...] * scale
    r.filt_two[...] = r.filter_two[...] * scale
    r.put(r.filt_one, r.filt_two)
    r.phi_own[...] = dot3(silu_parts(dot3(r.embedding[...], r.w_one_in))[0], r.w_one_out)
    r.put(r.phi_own)
    r.acc[...] = jnp.zeros_like(r.acc)
    first_messages(
        r.acc,
        r.geo_own,
        r.osc_own,
        r.state,
        r.work,
        r.gs,
        r.gv,
        r.phi_own,
        r.filt_one,
        own_rows,
        chunks,
    )
    r.put(r.acc)


def first_ghost_kernel(sizes, chunks, r):
    own_rows = r.embedding.shape[0]
    channels = r.embedding.shape[1]
    r.table[...] = jnp.zeros_like(r.table)
    arrival = receive(r, r.table, sizes)
    r.need(r.w_one_in, r.w_one_out, r.cols, r.mask_ghost)
    arrival()
    r.coords_ghost[...] = r.table[:, channels:]
    r.put(r.coords_ghost)
    r.phi_ghost[...] = dot3(
        silu_parts(dot3(r.table[:, :channels], r.w_one_in))[0], r.w_one_out
    )
    r.put(r.phi_ghost)
    members = r.mask_ghost.shape[0]
    geometry_by_atom(
        r.geo, r.osc, r.cols[...], ghost_lanes(r.coords_ghost), r.mask_ghost[...], r.wbox
    )
    r.need(r.acc, r.filt_one)
    first_messages(
        r.acc,
        r.geo,
        r.osc,
        r.state,
        r.work,
        r.gs,
        r.gv,
        r.phi_ghost,
        r.filt_one,
        members,
        chunks,
    )
    r.need(r.w_left, r.w_right, r.embedding, r.w_two_in, r.w_two_out, r.send_rows)
    top = 2 * own_rows
    half = 3 * own_rows
    acc, maps = r.acc, r.maps
    ah, al = split(acc[top:, :])
    maps[0 : 2 * half, :] = three(ah, al, *split(r.w_left[...]))
    maps[2 * half :, :] = three(ah, al, *split(r.w_right[...]))
    r.put(r.maps)
    total = r.embedding[...] + acc[0:own_rows, :]
    moved = acc[own_rows:top, :]
    for i in range(3):
        a, b = i * own_rows, (i + 1) * own_rows
        left, left_dot = maps[a:b, :], maps[half + a : half + b, :]
        right = maps[2 * half + a : 2 * half + b, :]
        right_dot = maps[3 * half + a : 3 * half + b, :]
        total = total + left * right
        moved = moved + left_dot * right + left * right_dot
    r.node[0:own_rows, :] = total
    r.node[own_rows:, :] = moved
    r.put(r.node)
    r.inner[...] = dot3(r.node[...], r.w_two_in)
    r.put(r.inner)
    value, slope, _ = silu_parts(r.inner[0:own_rows, :])
    outer = dot3(jnp.concatenate([value, slope * r.inner[own_rows:, :]], 0), r.w_two_out)
    r.phi_two[:, :channels] = outer[:own_rows]
    r.phi_two[:, channels:] = outer[own_rows:]
    r.put(r.phi_two)
    send_gathered(r, r.phi_two, r.stage, r.send_rows, sizes)


def ghost_lanes(coords):
    members = coords.shape[0]
    return jnp.concatenate([coords[...]] * (lanes // members), 0).T[:, :members]


def second_own_kernel(chunks, ghost_chunks, r):
    own_rows = r.mask_own.shape[0]
    ghosts = r.mask_ghost.shape[0]
    channels = r.filt_two.shape[1]
    r.acc_two[...] = jnp.zeros_like(r.acc_two)
    r.need(r.geo_own, r.osc_own, r.filt_two, r.phi_two)

    start_state(r.state, r.osc_own, own_rows)

    def own_basis(step, slot):
        kept = at(r.work, slot)
        plain_basis(kept, r.geo_own, r.osc_own, r.state, own_rows, step, own_rows)
        return kept

    second_messages(r.acc_two, own_basis, r.plain, r.dotted, r.filt_two, r.phi_two, chunks)
    r.put(r.acc_two)
    r.need(r.box, r.cols, r.mask_own, r.mask_ghost, r.coords_ghost)
    geometry_by_slot(
        r.geo, r.osc, r.coords_ghost[...], r.box[...], r.mask_ghost[...], r.wbox
    )
    start_state(r.state, r.osc, ghosts)
    steps(
        chunks,
        own_rows,
        lambda step, slot: plain_basis(
            at(r.at_ghost, step), r.geo, r.osc, r.state, own_rows, step, ghosts
        ),
    )
    r.put(r.at_ghost)
    geometry_by_atom(
        r.geo_ghost,
        r.osc,
        r.cols[...],
        ghost_lanes(r.coords_ghost),
        r.mask_ghost[...],
        r.wbox,
    )
    r.put(r.geo_ghost)
    start_state(r.state, r.osc, own_rows)
    steps(
        ghost_chunks,
        ghosts,
        lambda step, slot: plain_basis(
            at(r.a_ghost, step), r.geo_ghost, r.osc, r.state, ghosts, step, own_rows
        ),
    )
    r.put(r.a_ghost)
    r.need(r.phi_ghost, r.filt_one)
    start_state(r.state, r.osc, own_rows)

    def kept_for_back(step, slot):
        full_basis(r.basis_ghost.at[step], r.geo_ghost, r.osc, r.state, ghosts, step)
        phi = r.phi_ghost
        scaled_rows(r.gs_ghost, step, step, r.filt_one, slice(0, channels), phi[:, :channels])
        scaled_rows(
            r.gv_ghost, step, step, r.filt_one, slice(channels, None), phi[:, channels:]
        )

    steps(ghost_chunks, ghosts, kept_for_back)
    r.put(r.basis_ghost, r.gs_ghost, r.gv_ghost)


def second_ghost_kernel(sizes, chunks, ghost_chunks, r):
    own_rows = r.node.shape[0] // 2
    r.table[...] = jnp.zeros_like(r.table)
    arrival = receive(r, r.table, sizes)
    r.need(r.filt_two, r.acc_two)
    arrival()
    r.put(r.table)

    r.need(r.a_ghost)
    second_messages(
        r.acc_two,
        lambda step, slot: at(r.a_ghost, step),
        r.plain,
        r.dotted,
        r.filt_two,
        r.table,
        ghost_chunks,
    )
    r.need(r.node, r.w_hidden, r.w_energy)
    hidden = dot3(r.node[...] + r.acc_two[...], r.w_hidden)
    _, slope, bend = silu_parts(hidden[:own_rows])
    live = lax.broadcasted_iota(jnp.int32, (own_rows, 1), 0) < r.counts[0]
    weight = jnp.where(live, r.w_energy[...], 0.0)
    bars = jnp.concatenate([weight * slope, weight * bend * hidden[own_rows:]], 0)
    r.cot[...] = dot3(bars, r.w_hidden, nt_dims)
    r.put(r.cot)
    r.need(r.at_ghost)
    table_cotangents(
        r.back_ghost,
        lambda step, slot: at(r.at_ghost, step),
        r.plain,
        r.dotted,
        r.filt_two,
        r.cot,
        chunks,
    )
    send_groups(r, r.back_ghost, sizes)


def second_back_kernel(chunks, ghost_chunks, r):
    own_rows = r.mask_own.shape[0]
    r.need(r.box, r.cols, r.mask_own)
    geometry_by_slot(r.geo, r.osc, r.cols[...], r.box[...], r.mask_own[...], r.wbox)
    r.need(r.cot, r.filt_two)

    start_state(r.state, r.osc, own_rows)

    def slot_basis(step, slot):
        kept = at(r.work, slot)
        plain_basis(kept, r.geo, r.osc, r.state, own_rows, step, own_rows)
        return kept

    table_cotangents(r.back, slot_basis, r.plain, r.dotted, r.filt_two, r.cot, chunks)
    r.put(r.back)
    split_cot = at(r.work, 0)
    put_split(split_cot, 0, r.cot[...])
    r.need(r.geo_own, r.osc_own, r.phi_two)

    start_state(r.state, r.osc_own, own_rows)

    def own_basis(step, slot):
        kept = r.basis.at[slot]
        full_basis(kept, r.geo_own, r.osc_own, r.state, own_rows, step)
        return kept

    second_pairs(
        r.pair,
        r.pair_own,
        split_cot,
        own_basis,
        r.plain,
        r.dotted,
        r.filt_two,
        r.phi_two,
        chunks,
    )
    r.put(r.pair_own)
    r.need(r.table, r.basis_ghost)

    second_pairs(
        r.pair,
        r.pair_ghost,
        split_cot,
        lambda step, slot: r.basis_ghost.at[step],
        r.plain,
        r.dotted,
        r.filt_two,
        r.table,
        ghost_chunks,
    )
    r.put(r.pair_ghost)


def first_back_ghost_kernel(sizes, r):
    own_rows = r.back.shape[0]
    channels = r.back.shape[1] // 2
    arrival = receive(r, r.table, sizes)
    r.need(r.send_rows, r.back)
    arrival()
    add_returned(r.back, r.table, r.send_rows, sizes)
    r.need(r.w_two_out, r.inner, r.w_two_in, r.cot)
    outer = dot3(
        jnp.concatenate([r.back[:, :channels], r.back[:, channels:]], 0), r.w_two_out, nt_dims
    )
    _, slope, bend = silu_parts(r.inner[:own_rows, :])
    pulled = jnp.concatenate(
        [
            outer[:own_rows] * slope,
            outer[own_rows:] * slope + outer[:own_rows] * bend * r.inner[own_rows:, :],
        ],
        0,
    )
    bars = r.cot[...] + dot3(pulled, r.w_two_in, nt_dims)
    put_split(r.bars, 0, bars)
    half = 3 * own_rows
    maps = r.maps
    bar, bar_dot = bars[0:own_rows], bars[own_rows:]
    r.need(r.maps, r.w_left, r.w_right)
    for i in range(3):
        a, b = i * own_rows, (i + 1) * own_rows
        left, left_dot = maps[a:b, :], maps[half + a : half + b, :]
        right = maps[2 * half + a : 2 * half + b, :]
        right_dot = maps[3 * half + a : 3 * half + b, :]
        for_left = jnp.concatenate([bar * right, bar_dot * right + bar * right_dot], 0)
        for_right = jnp.concatenate([bar * left, bar_dot * left + bar * left_dot], 0)
        both = dot3(for_left, r.w_left, nt_dims) + dot3(for_right, r.w_right, nt_dims)
        put_split(r.bars, (2 + i) * own_rows, both[:own_rows])
        put_split(r.bars, (5 + i) * own_rows, both[own_rows:])
    r.put(r.bars)
    r.need(r.geo_ghost, r.gs_ghost, r.gv_ghost, r.basis_ghost)
    first_pairs(
        r.pair,
        r.cots,
        r.bars,
        r.geo_ghost,
        lambda step, slot: r.basis_ghost.at[step],
        lambda step, slot: (at(r.gs_ghost, step), at(r.gv_ghost, step)),
        r.table.shape[0],
        r.basis_ghost.shape[0],
    )
    r.by_slot[...] = jnp.zeros_like(r.by_slot)
    r.need(r.pair_ghost)
    members = r.table.shape[0]
    offset_gradients(r.geo_ghost, r.pair, r.pair_ghost, members, r.by_slot, r.by_atom)
    r.put(r.by_atom)
    send_chunks(r, lambda number: r.by_slot, sizes)


def first_back_own_kernel(chunks, r):
    own_rows = r.by_atom.shape[0]
    channels = r.phi_own.shape[1] // 2
    r.need(r.phi_own, r.filt_one, r.geo_own, r.osc_own, r.bars)

    start_state(r.state, r.osc_own, own_rows)

    def basis_at(step, slot):
        kept = r.basis.at[slot]
        full_basis(kept, r.geo_own, r.osc_own, r.state, own_rows, step)
        return kept

    def factors_at(step, slot):
        phi, filt = r.phi_own, r.filt_one
        scaled_rows(r.gs, slot, step, filt, slice(0, channels), phi[:, :channels])
        scaled_rows(r.gv, slot, step, filt, slice(channels, None), phi[:, channels:])
        return at(r.gs, slot), at(r.gv, slot)

    first_pairs(r.pair, r.cots, r.bars, r.geo_own, basis_at, factors_at, own_rows, chunks)
    r.result[...] = jnp.zeros_like(r.result)
    r.need(r.pair_own, r.by_atom)
    offset_gradients(r.geo_own, r.pair, r.pair_own, own_rows, r.result, r.atoms)
    r.result[...] += (r.atoms[...] + r.by_atom[...]).T[0:8, :]
    r.put(r.result)


def finish_kernel(sizes, r):
    count = r.send_rows.shape[1] // 8
    own_rows = r.result.shape[1]
    r.table[...] = jnp.zeros_like(r.table)
    arrival = receive(r, r.table, sizes)
    lane = lax.broadcasted_iota(jnp.int32, (1, lanes), 1)
    r.need(r.send_rows, r.result)
    atom = lax.broadcasted_iota(jnp.int32, (own_rows, 8 * count), 0)
    place = jnp.where(atom == r.send_rows[...], 1.0, 0.0).astype(bf16)
    arrival()
    rows = jnp.zeros((8, lanes), f32)
    for number in range(8):
        shift = ((2 * number - 7) * count) % lanes
        moved = r.table[8 * number : 8 * number + 8, :]
        if shift:
            moved = pltpu.roll(moved, shift, 1)
        mine = (lane >= number * count) & (lane < (number + 1) * count)
        rows = jnp.where(mine, moved, rows)
    value = rows[:, : 8 * count]
    high, low = split(value)
    rest = (value - high.astype(f32) - low.astype(f32)).astype(bf16)
    total = r.result[...] + mxu(high, place, nt_dims) + mxu(low, place, nt_dims)
    total = total + mxu(rest, place, nt_dims)
    r.forces[...] = -total[0:3, :]
    r.product[...] = -total[3:6, :]
    r.put(r.forces, r.product)


class Refs:
    def need(self, *buffers):
        for buffer in buffers:
            for copy in self.loads.pop(id(buffer), ()):
                copy.wait()

    def put(self, *buffers):
        for buffer in buffers:
            for copy in self.stores[id(buffer)]:
                copy.start()
                self.started.append(copy)

    def close(self):
        for copy in [copy for group in self.loads.values() for copy in group] + self.started:
            copy.wait()


def as_tuple(value):
    return value if isinstance(value, tuple) else (value,)


class Slot:
    def __init__(self, name, value):
        self.name, self.arrays = name, as_tuple(value)


class Slots:
    def __setattr__(self, name, value):
        object.__setattr__(self, name, Slot(name, value))


def call(kernel, v, loads, outs, scratch, index=(), raw=(), scalars=(), sent=()):
    args, kinds, shapes, buffers = [], [], [], []
    copied = [(slot, pltpu.VMEM) for slot in loads] + [(slot, pltpu.SMEM) for slot in index]
    copies = 0
    for slot, space in copied:
        for array in slot.arrays:
            args.append(pltpu.with_memory_space_constraint(array, pltpu.HBM))
            kinds.append(pl.BlockSpec(memory_space=pltpu.HBM))
            buffers.append(space(array.shape, array.dtype))
            copies += 1
    for slot in raw + scalars:
        args.append(slot.arrays[0])
        kinds.append(pl.BlockSpec(memory_space=pl.ANY if slot in raw else pltpu.SMEM))
    for shape, types in outs.values():
        for kind in as_tuple(types):
            shapes.append(pltpu.HBM(shape, kind))
            buffers.append(pltpu.VMEM(shape, kind))
            copies += 1
    if sent:
        shapes.append(pltpu.HBM(sent, f32))
    for shape, types in scratch.values():
        for kind in as_tuple(types):
            buffers.append(pltpu.VMEM(shape, kind))
    buffers.append(pltpu.SemaphoreType.DMA((copies + 1,)))
    buffers.append(pltpu.SemaphoreType.DMA((8,)))

    def run(*refs):
        r = Refs()
        r.loads, r.stores, r.started = {}, {}, []
        ins, refs = refs[: len(args)], refs[len(args) :]
        targets, refs = refs[: len(shapes)], list(refs[len(shapes) :])
        ins, targets = list(ins), list(targets)
        r.moves = refs[-1]
        sems = [refs[-2].at[number] for number in range(copies)]

        def taken(name, number):
            group = tuple(refs.pop(0) for _ in range(number))
            value = group if number > 1 else group[0]
            setattr(r, name, value)
            return group, id(value)

        for slot, _ in copied:
            group, key = taken(slot.name, len(slot.arrays))
            r.loads[key] = []
            for buffer in group:
                copy = pltpu.make_async_copy(ins.pop(0), buffer, sems.pop(0))
                copy.start()
                r.loads[key].append(copy)
        for slot in raw + scalars:
            setattr(r, slot.name, ins.pop(0))
        for name, (shape, types) in outs.items():
            group, key = taken(name, len(as_tuple(types)))
            r.stores[key] = []
            for buffer in group:
                copy = pltpu.make_async_copy(buffer, targets.pop(0), sems.pop(0))
                r.stores[key].append(copy)
        if sent:
            r.out = targets.pop(0)
        for name, (shape, types) in scratch.items():
            taken(name, len(as_tuple(types)))
        kernel(r)
        r.close()

    results = pl.pallas_call(
        run,
        out_shape=shapes,
        in_specs=kinds,
        out_specs=[pl.BlockSpec(memory_space=pltpu.HBM) for _ in shapes],
        scratch_shapes=buffers,
        compiler_params=pltpu.CompilerParams(vmem_limit_bytes=48 * 1024 * 1024),
        name=kernel.func.__name__,
    )(*args)
    results = list(results)
    for name, (shape, types) in outs.items():
        group = tuple(results.pop(0) for _ in as_tuple(types))
        setattr(v, name, group)
    if sent:
        v.arrived = exchanged(results.pop(0))


def exchanged(buffer):
    return lax.all_to_all(buffer, ("bx", "by"), 0, 0)


def per_device(
    positions,
    tangent,
    embedding,
    counts,
    neighbours,
    send_rows,
    w_one_in,
    w_one_out,
    filter_one,
    w_left,
    w_right,
    w_two_in,
    w_two_out,
    filter_two,
    w_hidden,
    w_energy,
):
    w_energy = w_energy.reshape(1, w_energy.shape[0])
    v = Slots()
    for name, value in tuple(locals().items()):
        if value is not v:
            setattr(v, name, value)
    sizes = (lax.axis_size("bx"), lax.axis_size("by"))
    devices = sizes[0] * sizes[1]
    n = positions.shape[1]
    channels = embedding.shape[1]
    ghosts = send_rows.shape[1]
    orders = filter_one.shape[0]
    count = ghosts // 8
    scale = 1.0 / math.sqrt(neighbours.shape[0])
    part = functools.partial
    pair = (bf16, bf16)
    own_chunks, ghost_chunks = orders * n // wide, orders * ghosts // wide

    def factors(chunks):
        return ((chunks, wide, channels), pair)

    geometry = ((geo_slots, n, wide), f32)
    osc = ((osc_slots, n, wide), f32)
    state = ((2, n, wide), f32)
    wbox = ((n, wide), f32)
    pairs = ((8, n, wide), f32)
    cots = ((2, 8 * n, wide), f32)

    call(
        part(pack_kernel, sizes),
        v,
        (v.positions, v.tangent, v.embedding),
        dict(),
        dict(
            box=((n, n), f32),
            table=((n, channels + lanes), f32),
            stage=((ghosts, channels + lanes), f32),
        ),
        index=(v.send_rows,),
        sent=(devices, count, channels + lanes),
    )
    call(
        part(first_own_kernel, scale, own_chunks),
        v,
        (v.positions, v.tangent, v.neighbours, v.w_one_in, v.w_one_out, v.embedding, v.filter_one, v.filter_two),
        dict(
            box=((n, n), f32),
            cols=((n, n), f32),
            mask_own=((n, n), f32),
            mask_ghost=((ghosts, n), f32),
            filt_one=((orders, 2 * channels), f32),
            filt_two=((orders, channels), f32),
            acc=((8 * n, channels), f32),
            geo_own=geometry,
            osc_own=osc,
            phi_own=((n, 2 * channels), f32),
        ),
        dict(
            gs=factors(2),
            gv=factors(2),
            wbox=wbox,
            state=state,
            work=((2, 8 * n, wide), pair),
        ),
    )
    call(
        part(first_ghost_kernel, sizes, ghost_chunks),
        v,
        (v.w_one_in, v.cols, v.mask_ghost, v.w_one_out, v.filt_one, v.acc, v.w_left, v.w_right, v.embedding, v.w_two_in, v.w_two_out),
        dict(
            node=((2 * n, channels), f32),
            inner=((2 * n, channels), f32),
            maps=((12 * n, channels), f32),
            phi_two=((n, 2 * channels), f32),
            phi_ghost=((ghosts, 2 * channels), f32),
            coords_ghost=((ghosts, lanes), f32),
        ),
        dict(
            geo=geometry,
            osc=osc,
            gs=factors(2),
            gv=factors(2),
            wbox=wbox,
            state=state,
            work=((2, 8 * n, wide), pair),
            table=((ghosts, channels + lanes), f32),
            stage=((ghosts, 2 * channels), f32),
        ),
        index=(v.send_rows,),
        raw=(v.arrived,),
        sent=(devices, count, 2 * channels),
    )
    call(
        part(second_own_kernel, own_chunks, ghost_chunks),
        v,
        (v.geo_own, v.osc_own, v.phi_two, v.filt_two, v.box, v.cols, v.mask_own, v.mask_ghost, v.coords_ghost, v.phi_ghost, v.filt_one),
        dict(
            acc_two=((2 * n, channels), f32),
            at_ghost=((own_chunks, 2 * ghosts, wide), pair),
            geo_ghost=geometry,
            a_ghost=((ghost_chunks, 2 * n, wide), pair),
            basis_ghost=((ghost_chunks, 3, n, wide), f32),
            gs_ghost=factors(ghost_chunks),
            gv_ghost=factors(ghost_chunks),
        ),
        dict(
            geo=geometry,
            osc=osc,
            state=state,
            wbox=wbox,
            work=((2, 2 * n, wide), pair),
            plain=factors(2),
            dotted=factors(2),
        ),
    )
    call(
        part(second_ghost_kernel, sizes, own_chunks, ghost_chunks),
        v,
        (v.filt_two, v.acc_two, v.a_ghost, v.node, v.w_hidden, v.w_energy, v.at_ghost),
        dict(
            cot=((2 * n, channels), f32),
            table=((ghosts, 2 * channels), f32),
        ),
        dict(
            plain=factors(2),
            dotted=factors(2),
            back_ghost=((ghosts, 2 * channels), f32),
        ),
        raw=(v.arrived,),
        scalars=(v.counts,),
        sent=(devices, count, 2 * channels),
    )
    call(
        part(second_back_kernel, own_chunks, ghost_chunks),
        v,
        (v.box, v.cols, v.mask_own, v.cot, v.filt_two, v.geo_own, v.osc_own, v.phi_two, v.table, v.basis_ghost),
        dict(
            back=((n, 2 * channels), f32),
            pair_own=((2, n, lanes), f32),
            pair_ghost=((2, n, lanes), f32),
        ),
        dict(
            basis=((2, 3, n, wide), f32),
            geo=geometry,
            osc=osc,
            state=state,
            wbox=wbox,
            work=((2, 2 * n, wide), pair),
            plain=factors(2),
            dotted=factors(2),
            pair=((2, n, wide), f32),
        ),
    )
    call(
        part(first_back_ghost_kernel, sizes),
        v,
        (v.back, v.w_two_out, v.inner, v.w_two_in, v.cot, v.maps, v.w_left, v.w_right, v.geo_ghost, v.gs_ghost, v.gv_ghost, v.basis_ghost, v.pair_ghost),
        dict(
            bars=((8 * n, channels), pair),
            by_atom=((n, lanes), f32),
        ),
        dict(
            table=((ghosts, 2 * channels), f32),
            by_slot=((8, lanes), f32),
            pair=pairs,
            cots=cots,
        ),
        index=(v.send_rows,),
        raw=(v.arrived,),
        sent=(devices, 8, lanes),
    )
    call(
        part(first_back_own_kernel, own_chunks),
        v,
        (v.phi_own, v.filt_one, v.geo_own, v.osc_own, v.bars, v.pair_own, v.by_atom),
        dict(result=((8, lanes), f32)),
        dict(
            atoms=((n, lanes), f32),
            pair=pairs,
            cots=cots,
            state=state,
            gs=factors(2),
            gv=factors(2),
            basis=((2, 3, n, wide), f32),
        ),
    )
    call(
        part(finish_kernel, sizes),
        v,
        (v.send_rows, v.result),
        dict(forces=((3, n), f32), product=((3, n), f32)),
        dict(table=((64, lanes), f32)),
        raw=(v.arrived,),
    )
    return v.forces.arrays[0], v.product.arrays[0]


def solution(mesh):
    brick = ("bx", "by")
    placed = (
        P(None, brick),
        P(None, brick),
        P(brick, None),
        P(brick),
        P(None, brick),
        P(brick, None),
    ) + (P(),) * 10

    return jax.shard_map(
        per_device,
        mesh=mesh,
        in_specs=placed,
        out_specs=(P(None, brick), P(None, brick)),
        check_vma=False,
    )
```

profile of v0, /device:TPU:4, one launch (start us, length us, event | category | flops | bytes accessed | tf_op | source)
XLA Modules:
  0.0 96.3 jit_solution(9701854465542236955)
XLA Ops:
  0.6 1.8 %pack_kernel.1 = f32[32,8,384]{2,1,0:T(8,128)} custom-call(f32[3,128]{1,0:T(4,128)} %refs_0_.5, f32[3,128]{1,0:T(4,128)} %refs_1_.4, f32[128,256]{1,0:T(8,128)} %refs_8_.1, s32[1,64]{1,0:T(1,128)} %refs_0_.7), custom_call_target="tpu_custom_call" | custom-call | tf_op jit(solution)/shard_map/pack_kernel/pallas_call | solution.py:949
  2.5 6.1 %all-to-all-start = ((f32[32,8,384]{2,1,0:T(8,128)}), f32[32,8,384]{2,1,0:T(8,128)S(1)}, u32[]{:S(2)}, u32[]{:S(2)}) async-start(f32[32,8,384]{2,1,0:T(8,128)} %pack_kernel.1), calls=%async_computation | async-start | bytes 786432 | tf_op jit(solution)/shard_map/all_to_all | solution.py:967
  8.6 9.0 %first_own_kernel.1 = (f32[128,128]{1,0:T(8,128)}, f32[128,128]{1,0:T(8,128)}, f32[128,128]{1,0:T(8,128)}, f32[64,128]{1,0:T(8,128)}, f32[20,512]{1,0:T(8,128)},...) custom-call(f32[3,128]{1,0:T(4,128)} %refs_0_.5, ...), custom_call_target="tpu_custom_call" | custom-call | tf_op jit(solution)/shard_map/first_own_kernel/pallas_call | solution.py:949
  17.5 3.4 %all-to-all-done.refs_12_ = f32[32,8,384]{2,1,0:T(8,128)S(1)} async-done(((f32[32,8,384]{2,1,0:T(8,128)}), f32[32,8,384]{2,1,0:T(8,128)S(1)}, u32[]{:S(2)}, u32[]{:S(2)}) %all-to-all-start) | async-done | bytes 393248 | tf_op jit(solution)/shard_map/all_to_all | solution.py:967
  21.0 8.6 %first_ghost_kernel.1 = (f32[256,256]{1,0:T(8,128)}, f32[256,256]{1,0:T(8,128)}, f32[1536,256]{1,0:T(8,128)}, f32[128,512]{1,0:T(8,128)}, f32[64,512]{1,0:T(8,12...) custom-call(f32[256,256]{1,0:T(8,128)} %refs_0_.6, f32[128,128]{1,0:T(8,128)} %get-tuple-element.45.refs_1_.refs_5_, ...), custom_call_target="tpu_custom_call" | custom-call | tf_op jit(solution)/shard_map/first_ghost_kernel/pallas_call | solution.py:949
  29.6 3.4 %all-to-all-start.1 = ((f32[32,8,512]{2,1,0:T(8,128)}), f32[32,8,512]{2,1,0:T(8,128)S(1)}, u32[]{:S(2)}, u32[]{:S(2)}) async-start(f32[32,8,512]{2,1,0:T(8,128)} %get-tuple-element.59), calls=%async_computation.1 | async-start | bytes 1048576 | tf_op jit(solution)/shard_map/all_to_all | solution.py:967
  33.6 9.3 %second_own_kernel.1 = (f32[256,256]{1,0:T(8,128)}, bf16[10,128,256]{2,1,0:T(8,128)(2,1)}, bf16[10,128,256]{2,1,0:T(8,128)(2,1)}, f32[8,128,256]{2,1,0:T(8,128)}...) custom-call(f32[8,128,256]{2,1,0:T(8,128)} %get-tuple-element.42.ref, ...), custom_call_target="tpu_custom_call" | custom-call | tf_op jit(solution)/shard_map/second_own_kernel/pallas_call | solution.py:949
  42.9 5.1 %all-to-all-done.1.refs_9_ = f32[32,8,512]{2,1,0:T(8,128)S(1)} async-done(((f32[32,8,512]{2,1,0:T(8,128)}), f32[32,8,512]{2,1,0:T(8,128)S(1)}, u32[]{:S(2)}, u32[]{:S(2)}) %all-to-all-start.1) | async-done | bytes 524320 | tf_op jit(solution)/shard_map/all_to_all | solution.py:967
  48.0 6.5 %second_ghost_kernel.1 = (f32[256,256]{1,0:T(8,128)}, f32[64,512]{1,0:T(8,128)}, f32[32,8,512]{2,1,0:T(8,128)}) custom-call(f32[20,256]{1,0:T(8,128)} %get-tuple-element.47.refs_3_.refs_0_.refs_4_, f32[256,256]{1,0:T(8,128)} %get-tuple-element.53.refs_1_, bf16[5,256,256]{2,1,0:T(8,128)(2,1)} %get-tuple-element.54.refs_2_, ...), custom_call_target="tpu_custom_call" | custom-call | tf_op jit(solution)/shard_map/second_ghost_kernel/pallas_call | solution.py:949
  54.5 3.6 %all-to-all-start.2 = ((f32[32,8,512]{2,1,0:T(8,128)}), f32[32,8,512]{2,1,0:T(8,128)S(1)}, u32[]{:S(2)}, u32[]{:S(2)}) async-start(f32[32,8,512]{2,1,0:T(8,128)} %get-tuple-element.72), calls=%async_computation.2 | async-start | bytes 1048576 | tf_op jit(solution)/shard_map/all_to_all | solution.py:967
  58.2 10.5 %second_back_kernel.1 = (f32[128,512]{1,0:T(8,128)}, f32[2,128,128]{2,1,0:T(8,128)}, f32[2,128,128]{2,1,0:T(8,128)}) custom-call(f32[128,128]{1,0:T(8,128)} %get-tuple-element.44.refs_4_.refs_0_, f32[128,128]{1,0:T(8,128)} %get-tuple-element.45.refs_1_.refs_5_, f32[128,128]{1,0:T(8,128)} %get-tuple-element.46.refs_6_.refs_2_, ...), custom_call_target="tpu_custom_call" | custom-call | tf_op jit(solution)/shard_map/second_back_kernel/pallas_call | solution.py:949
  68.7 4.5 %all-to-all-done.2.refs_16_ = f32[32,8,512]{2,1,0:T(8,128)S(1)} async-done(((f32[32,8,512]{2,1,0:T(8,128)}), f32[32,8,512]{2,1,0:T(8,128)S(1)}, u32[]{:S(2)}, u32[]{:S(2)}) %all-to-all-start.2) | async-done | bytes 524320 | tf_op jit(solution)/shard_map/all_to_all | solution.py:967
  73.2 8.0 %first_back_ghost_kernel.1 = (bf16[1024,256]{1,0:T(8,128)(2,1)}, bf16[1024,256]{1,0:T(8,128)(2,1)}, f32[128,128]{1,0:T(8,128)}, f32[32,8,128]{2,1,0:T(8,128)}) custom-call(f32[128,512]{1,0:T(8,128)} %get-tuple-element.63.refs_0_, f32[256,256]{1,0:T(8,128)} %refs_1_.5, f32[256,256]{1,0:T(8,128)} %get-tuple-element.64.refs_2_, f32[256,256]{1,0:T(8,128)} %refs_3_.7, ...), custom_call_target="tpu_custom_call" | custom-call | tf_op jit(solution)/shard_map/first_back_ghost_kernel/pallas_call | solution.py:949
  81.2 3.6 %all-to-all-start.3 = ((f32[32,8,128]{2,1,0:T(8,128)}), f32[32,8,128]{2,1,0:T(8,128)S(1)}, u32[]{:S(2)}, u32[]{:S(2)}) async-start(f32[32,8,128]{2,1,0:T(8,128)} %get-tuple-element.77), calls=%async_computation.3 | async-start | bytes 262144 | tf_op jit(solution)/shard_map/all_to_all | solution.py:967
  84.8 9.8 %first_back_own_kernel.1.refs_1_ = f32[8,128]{1,0:T(8,128)} custom-call(f32[128,512]{1,0:T(8,128)} %get-tuple-element.40.refs_0_, f32[20,512]{1,0:T(8,128)} %get-tuple-element.41.refs_4_.refs_10_.refs_1_, f32[8,128,256]{2,1,0:T(8,128)} %get-tuple-element.42.refs_0_.refs_5_.refs_2_, f32[7,128,256]{2,1,0:T(8,128)} %get-tuple-element.43.refs_1_.refs_6_.refs_3_, ...), custom_call_target="tpu_custom_call" | custom-call | tf_op jit(solution)/shard_map/first_back_own_kernel/pallas_call | solution.py:949
  94.6 0.0 all-to-all-done.3.refs_2_
  94.6 1.6 %finish_kernel.1 = (f32[3,128]{1,0:T(4,128)}, f32[3,128]{1,0:T(4,128)}) custom-call(s32[1,64]{1,0:T(1,128)} %refs_0_.7, f32[8,128]{1,0:T(8,128)} %first_back_own_kernel.1.refs_1_, f32[32,8,128]{2,1,0:T(8,128)S(1)} %all-to-all-done.3.refs_2_), custom_call_target="tpu_custom_call" | custom-call | tf_op jit(solution)/shard_map/finish_kernel/pallas_call | solution.py:949
Async XLA Ops:
  2.5 18.5 %all-to-all-start = ((f32[32,8,384]{2,1,0:T(8,128)}), f32[32,8,384]{2,1,0:T(8,128)S(1)}, u32[]{:S(2)}, u32[]{:S(2)}) async-start(f32[32,8,384]{2,1,0:T(8,128)} %pack_kernel.1), calls=%async_computation | async-start | bytes 786432 | tf_op jit(solution)/shard_map/all_to_all | solution.py:967
  29.6 18.5 %all-to-all-start.1 = ((f32[32,8,512]{2,1,0:T(8,128)}), f32[32,8,512]{2,1,0:T(8,128)S(1)}, u32[]{:S(2)}, u32[]{:S(2)}) async-start(f32[32,8,512]{2,1,0:T(8,128)} %get-tuple-element.59), calls=%async_computation.1 | async-start | bytes 1048576 | tf_op jit(solution)/shard_map/all_to_all | solution.py:967
  54.5 18.7 %all-to-all-start.2 = ((f32[32,8,512]{2,1,0:T(8,128)}), f32[32,8,512]{2,1,0:T(8,128)S(1)}, u32[]{:S(2)}, u32[]{:S(2)}) async-start(f32[32,8,512]{2,1,0:T(8,128)} %get-tuple-element.72), calls=%async_computation.2 | async-start | bytes 1048576 | tf_op jit(solution)/shard_map/all_to_all | solution.py:967
  81.2 13.4 %all-to-all-start.3 = ((f32[32,8,128]{2,1,0:T(8,128)}), f32[32,8,128]{2,1,0:T(8,128)S(1)}, u32[]{:S(2)}, u32[]{:S(2)}) async-start(f32[32,8,128]{2,1,0:T(8,128)} %get-tuple-element.77), calls=%async_computation.3 | async-start | bytes 262144 | tf_op jit(solution)/shard_map/all_to_all | solution.py:967
where the time goes:
time: 98.1 us; the launch traced here: 96.3 us
  Pallas kernels  65 us (66%)
  starting transfers between devices  16.8 us (17%)
  waiting for transfers between devices  13 us (13%)
  between operations  1.54 us (2%)
    pallas_call x9, Pallas kernels, call(): pl.pallas_call(run, out_shape=shapes, in_specs=kinds, out_specs=[pl.Block...  65 us
    all_to_all x4, starting transfers between devices, exchanged(): return lax.all_to_all(buffer, ('bx', 'by'), 0, 0)  16.8 us
    all_to_all x4, waiting for transfers between devices, exchanged(): return lax.all_to_all(buffer, ('bx', 'by'), 0, 0)  13 us
  transfers between devices with their start and end apart: 4, of which 3 were waited for; matrix products, arithmetic and copies ran while one was open for 0% of the time, Pallas kernels for 40%

commit v1 on v0

--- a/solution.py
+++ b/solution.py
@@ -22,8 +22,8 @@
 
 U, UD, DD, RI = 0, 3, 6, 7
 geo_slots = 8
-P0, P1, P2, SN, CS, RS, RC = 0, 1, 2, 3, 4, 5, 6
-osc_slots = 7
+P0, P1, P2, SN, CS = 0, 1, 2, 3, 4
+osc_slots = 5
 own_group = 2
 ghost_group = 5
 
@@ -76,9 +76,11 @@
     return 2.0 * s * c, 1.0 - 2.0 * s * s
 
 
-def fill_geometry(geo, osc, first, second, mask_at, height, members):
-    repeats = wide // members
-    group = lax.broadcasted_iota(jnp.int32, (1, wide), 1) // members
+def doubled(value):
+    return jnp.concatenate([value, value], 1)
+
+
+def fill_geometry(geo, osc, first, second, mask_at, height):
     for start in range(0, height, row_block):
         rows = pl.ds(start, row_block)
         off = [first(i, start) - second(i, start) for i in range(3)]
@@ -98,20 +100,35 @@
         g2 = ((-0.5 * wave * wave) * cs - 2.0 * g1) * inverse
         mask = mask_at(start)
         geo[DD, rows, :] = speed
+        geo[RI, rows, :] = inverse
         osc[P0, rows, :] = mask * g0
         osc[P1, rows, :] = mask * g1
         osc[P2, rows, :] = mask * g2
-        geo[RI, rows, :] = inverse
-        turn_s, turn_c = sn, cs
-        state_s, state_c = sn, cs
-        for i in range(1, repeats):
-            turn_s, turn_c = turn_s * cs + turn_c * sn, turn_c * cs - turn_s * sn
-            state_s = jnp.where(group >= i, turn_s, state_s)
-            state_c = jnp.where(group >= i, turn_c, state_c)
-        osc[SN, rows, :] = state_s
-        osc[CS, rows, :] = state_c
-        osc[RS, rows, :] = turn_s
-        osc[RC, rows, :] = turn_c
+        osc[SN, rows, :] = sn
+        osc[CS, rows, :] = cs
+
+
+def start_state(state, osc, height, members):
+    waves, turn = state
+    near = lanes // members
+    group = lax.broadcasted_iota(jnp.int32, (1, lanes), 1) // members
+    for start in range(0, height, row_block):
+        rows = pl.ds(start, row_block)
+        sn, cs = osc[SN, rows, :], osc[CS, rows, :]
+        s, c = sn, cs
+        for half in range(wide // lanes):
+            place = pl.ds(half * lanes, lanes)
+            if half:
+                s, c = s * cs + c * sn, c * cs - s * sn
+            state_s, state_c = s, c
+            for i in range(1, near):
+                s, c = s * cs + c * sn, c * cs - s * sn
+                state_s = jnp.where(group >= i, s, state_s)
+                state_c = jnp.where(group >= i, c, state_c)
+            waves[0, rows, place] = state_s
+            waves[1, rows, place] = state_c
+        turn[0, rows, :] = s
+        turn[1, rows, :] = c
 
 
 def order_factor(step, members):
@@ -120,11 +137,12 @@
     return (group + (step * repeats + 1)).astype(f32) * wave
 
 
-def rotate(wave_state, osc, rows, s, c):
-    rs = osc[RS, rows, :]
-    rc = osc[RC, rows, :]
-    wave_state[0, rows, :] = s * rc + c * rs
-    wave_state[1, rows, :] = c * rc - s * rs
+def rotate(state, rows, s, c):
+    waves, turn = state
+    rs = doubled(turn[0, rows, :])
+    rc = doubled(turn[1, rows, :])
+    waves[0, rows, :] = s * rc + c * rs
+    waves[1, rows, :] = c * rc - s * rs
 
 
 def steps(count, members, body):
@@ -142,11 +160,6 @@
     lax.fori_loop(0, count // group, several, 0)
 
 
-def start_state(state, osc, height):
-    state[0, 0:height, :] = osc[SN, 0:height, :]
-    state[1, 0:height, :] = osc[CS, 0:height, :]
-
-
 def listed(nbr_ref, start, members):
     slot = lax.broadcasted_iota(jnp.int32, (members, lanes), 0) + start
     found = nbr_ref[0:1, :] == slot
@@ -156,8 +169,7 @@
 
 
 def geometry_by_atom(geo, osc, columns, table, mask, wbox):
-    members = mask.shape[0]
-    repeats = wide // members
+    repeats = lanes // mask.shape[0]
     table = jnp.concatenate([table] * repeats, 1)
     wbox[...] = jnp.concatenate([mask] * repeats, 0).T
     fill_geometry(
@@ -167,23 +179,17 @@
         lambda i, start: columns[start : start + row_block, i : i + 1],
         lambda start: wbox[start : start + row_block, :],
         geo.shape[1],
-        members,
-    )
-
-
-def geometry_by_slot(geo, osc, columns, centre, mask, wbox):
-    height, own_rows = mask.shape
-    repeats = wide // own_rows
-    centre = jnp.concatenate([centre] * repeats, 1)
-    wbox[0:height, :] = jnp.concatenate([mask] * repeats, 1)
+    )
+
+
+def geometry_by_slot(geo, osc, columns, centre, mask):
     fill_geometry(
         geo,
         osc,
         lambda i, start: columns[start : start + row_block, i : i + 1],
         lambda i, start: centre[i : i + 1, :],
-        lambda start: wbox[start : start + row_block, :],
-        height,
-        own_rows,
+        lambda start: mask[start : start + row_block, :],
+        mask.shape[0],
     )
 
 
@@ -208,13 +214,13 @@
 
 def basis_rows(kept, state, geo, osc, step, factor, start, height):
     rows = pl.ds(start, row_block)
-    s, c = state[0, rows, :], state[1, rows, :]
-    p0 = osc[P0, rows, :]
+    s, c = state[0][0, rows, :], state[0][1, rows, :]
+    p0 = doubled(osc[P0, rows, :])
     b = p0 * s
-    bd = (osc[P1, rows, :] * s + factor * (p0 * c)) * geo[DD, rows, :]
+    bd = (doubled(osc[P1, rows, :]) * s + factor * (p0 * c)) * doubled(geo[DD, rows, :])
     put_split(kept, start, b)
     put_split(kept, height + start, bd)
-    rotate(state, osc, rows, s, c)
+    rotate(state, rows, s, c)
     return b, bd
 
 
@@ -222,7 +228,7 @@
     height = geo.shape[1]
     channels = phi.shape[1] // 2
     top = 2 * height
-    start_state(state, osc, height)
+    start_state(state, osc, height, members)
 
     def chunk(step, slot):
         factor = order_factor(step, members)
@@ -233,10 +239,10 @@
             rows = pl.ds(start, row_block)
             b, bd = basis_rows(now, state, geo, osc, step, factor, start, height)
             for i in range(3):
-                unit = geo[U + i, rows, :]
+                unit = doubled(geo[U + i, rows, :])
                 put_split(now, (2 + i) * height + start, unit * b)
                 put_split(
-                    now, (5 + i) * height + start, geo[UD + i, rows, :] * b + unit * bd
+                    now, (5 + i) * height + start, doubled(geo[UD + i, rows, :]) * b + unit * bd
                 )
         ah, al = now
         acc[:top, :] += three(ah[:top, :], al[:top, :], scalars[0][slot], scalars[1][slot])
@@ -267,20 +273,19 @@
         basis_rows(kept, state, geo, osc, step, factor, start, height)
 
 
-def full_basis(kept, geo, osc, state, members, step):
-    height = geo.shape[1]
+def full_basis(geo, osc, state, members, step):
     factor = order_factor(step, members)
-    for start in range(0, height, row_block):
-        rows = pl.ds(start, row_block)
-        s, c = state[0, rows, :], state[1, rows, :]
-        p0, p1 = osc[P0, rows, :], osc[P1, rows, :]
+
+    def at_rows(rows):
+        s, c = state[0][0, rows, :], state[0][1, rows, :]
+        p0, p1 = doubled(osc[P0, rows, :]), doubled(osc[P1, rows, :])
         b = p0 * s
-        kept[0, rows, :] = b
-        kept[1, rows, :] = p1 * s + factor * (p0 * c)
-        kept[2, rows, :] = (
-            osc[P2, rows, :] * s + factor * (2.0 * p1 * c - factor * b)
-        ) * geo[DD, rows, :]
-        rotate(state, osc, rows, s, c)
+        b1 = p1 * s + factor * (p0 * c)
+        b2 = doubled(osc[P2, rows, :]) * s + factor * (2.0 * p1 * c - factor * b)
+        rotate(state, rows, s, c)
+        return b, b1, b2 * doubled(geo[DD, rows, :])
+
+    return at_rows
 
 
 def table_cotangents(back, basis_at, plain, dotted, filt, cot, chunks):
@@ -322,13 +327,13 @@
         dot = both[height:] + three(
             ah[:height, :], al[:height, :], dotted[0][slot], dotted[1][slot], nt_dims
         )
-        basis = basis_at(step, slot)
+        basis = basis_at(step)
         for start in range(0, height, row_block):
             rows = pl.ds(start, row_block)
-            b1 = basis[1, rows, :]
+            _, b1, b2d = basis(rows)
             g = both[start : start + row_block]
             pair[0, rows, :] += b1 * g
-            pair[1, rows, :] += basis[2, rows, :] * g + b1 * dot[start : start + row_block]
+            pair[1, rows, :] += b2d * g + b1 * dot[start : start + row_block]
 
     members = value.shape[0]
     steps(chunks, members, chunk)
@@ -351,11 +356,11 @@
         cots[top:, :] = three(
             ch[top:, :], cl[top:, :], vectors[0][...], vectors[1][...], nt_dims
         )
-        basis = basis_at(step, slot)
+        basis = basis_at(step)
         for start in range(0, height, row_block):
             rows = pl.ds(start, row_block)
-            b, b1, b2d = [basis[i, rows, :] for i in range(3)]
-            b1d = b1 * geo[DD, rows, :]
+            b, b1, b2d = basis(rows)
+            b1d = b1 * doubled(geo[DD, rows, :])
             along = cots[start : start + row_block, :]
             along_dot = cots[height + start : height + start + row_block, :]
             for i in range(3):
@@ -363,9 +368,9 @@
                 g = cots[place : place + row_block, :]
                 place = (5 + i) * height + start
                 gd = cots[place : place + row_block, :]
-                unit = geo[U + i, rows, :]
+                unit = doubled(geo[U + i, rows, :])
                 along = along + unit * g
-                along_dot = along_dot + unit * gd + geo[UD + i, rows, :] * g
+                along_dot = along_dot + unit * gd + doubled(geo[UD + i, rows, :]) * g
                 pair[2 + i, rows, :] += b * g
                 pair[5 + i, rows, :] += b * gd + b1d * g
             pair[0, rows, :] += b1 * along
@@ -413,33 +418,20 @@
 
 def receive(r, table, sizes):
     count = r.arrived.shape[1]
-
-    def each(act):
-        for number, target in enumerate(offsets):
-            device, inside = neighbour_id(target, sizes)
-            copy = pltpu.make_async_copy(
-                r.arrived.at[device],
-                table.at[number * count : (number + 1) * count, :],
-                r.moves.at[number],
-            )
-
-            @pl.when(inside)
-            def _():
-                act(copy)
-
-    each(lambda copy: copy.start())
-    return lambda: each(lambda copy: copy.wait())
-
-
-def add_returned(total, table, send_ref, sizes):
-    count = table.shape[0] // 8
     for number, target in enumerate(offsets):
         device, inside = neighbour_id(target, sizes)
 
         @pl.when(inside)
         def _():
-            for slot in range(number * count, (number + 1) * count):
-                total[pl.ds(send_ref[0, slot], 1), :] += table[slot : slot + 1, :]
+            table[number * count : (number + 1) * count, :] = r.arrived[device]
+
+
+def add_returned(total, table, send_row):
+    atom = lax.broadcasted_iota(jnp.int32, (total.shape[0], table.shape[0]), 0)
+    place = jnp.where(atom == send_row, 1.0, 0.0).astype(bf16)
+    high, low = split(table[...])
+    rest = (table[...] - high.astype(f32) - low.astype(f32)).astype(bf16)
+    total[...] += mxu(place, high) + mxu(place, low) + mxu(place, rest)
 
 
 def offset_gradients(geo, pair, second, members, by_slot, by_atom):
@@ -484,7 +476,17 @@
     r.need(r.embedding)
     r.table[:, :channels] = r.embedding[...]
     r.need(r.send_rows)
-    send_gathered(r, r.table, r.stage, r.send_rows, sizes)
+    count = r.send_rows.shape[1] // 8
+    gap = lanes // count
+    for number in range(8):
+        ends = jnp.zeros((1, lanes), f32)
+        for p in range(count):
+            row = r.table[pl.ds(r.send_rows[0, number * count + p], 1), :]
+            r.stage[number, :, p * channels : (p + 1) * channels] = row[:, :channels]
+            end = row[:, channels:]
+            ends = ends + (pltpu.roll(end, p * gap, 1) if p else end)
+        r.stage[number, :, count * channels :] = ends
+    send_chunks(r, lambda number: r.stage.at[number], sizes)
 
 
 def first_own_kernel(scale, chunks, r):
@@ -497,12 +499,17 @@
     r.mask_own[...] = listed(r.neighbours, 0, own_rows)
     r.mask_ghost[...] = listed(r.neighbours, own_rows, r.mask_ghost.shape[0])
     r.put(r.box, r.cols, r.mask_own, r.mask_ghost)
+    r.cols_near[...] = r.cols[...]
+    r.mask_near[...] = r.mask_ghost[...]
     geometry_by_atom(r.geo_own, r.osc_own, r.cols[...], r.box[...], r.mask_own[...], r.wbox)
     r.put(r.geo_own, r.osc_own)
     r.need(r.w_one_in, r.w_one_out, r.embedding, r.filter_one, r.filter_two)
     r.filt_one[...] = r.filter_one[...] * scale
     r.filt_two[...] = r.filter_two[...] * scale
     r.put(r.filt_one, r.filt_two)
+    r.filt_near[...] = r.filt_one[...]
+    r.in_near[...] = r.w_one_in[...]
+    r.out_near[...] = r.w_one_out[...]
     r.phi_own[...] = dot3(silu_parts(dot3(r.embedding[...], r.w_one_in))[0], r.w_one_out)
     r.put(r.phi_own)
     r.acc[...] = jnp.zeros_like(r.acc)
@@ -519,27 +526,36 @@
         own_rows,
         chunks,
     )
-    r.put(r.acc)
 
 
 def first_ghost_kernel(sizes, chunks, r):
     own_rows = r.embedding.shape[0]
     channels = r.embedding.shape[1]
     r.table[...] = jnp.zeros_like(r.table)
-    arrival = receive(r, r.table, sizes)
-    r.need(r.w_one_in, r.w_one_out, r.cols, r.mask_ghost)
-    arrival()
+    count = r.table.shape[0] // 8
+    gap = lanes // count
+    for number, target in enumerate(offsets):
+        device, inside = neighbour_id(target, sizes)
+
+        @pl.when(inside)
+        def _():
+            chunk = r.arrived[device]
+            ends = chunk[:, count * channels :]
+            for p in range(count):
+                at_row = slice(number * count + p, number * count + p + 1)
+                r.table[at_row, :channels] = chunk[:, p * channels : (p + 1) * channels]
+                r.table[at_row, channels:] = pltpu.roll(ends, lanes - p * gap, 1) if p else ends
+
     r.coords_ghost[...] = r.table[:, channels:]
     r.put(r.coords_ghost)
     r.phi_ghost[...] = dot3(
-        silu_parts(dot3(r.table[:, :channels], r.w_one_in))[0], r.w_one_out
+        silu_parts(dot3(r.table[:, :channels], r.in_near))[0], r.out_near
     )
     r.put(r.phi_ghost)
-    members = r.mask_ghost.shape[0]
+    members = r.mask_near.shape[0]
     geometry_by_atom(
-        r.geo, r.osc, r.cols[...], ghost_lanes(r.coords_ghost), r.mask_ghost[...], r.wbox
-    )
-    r.need(r.acc, r.filt_one)
+        r.geo, r.osc, r.cols_near[...], ghost_lanes(r.coords_ghost), r.mask_near[...], r.wbox
+    )
     first_messages(
         r.acc,
         r.geo,
@@ -549,7 +565,7 @@
         r.gs,
         r.gv,
         r.phi_ghost,
-        r.filt_one,
+        r.filt_near,
         members,
         chunks,
     )
@@ -591,11 +607,11 @@
 def second_own_kernel(chunks, ghost_chunks, r):
     own_rows = r.mask_own.shape[0]
     ghosts = r.mask_ghost.shape[0]
-    channels = r.filt_two.shape[1]
     r.acc_two[...] = jnp.zeros_like(r.acc_two)
     r.need(r.geo_own, r.osc_own, r.filt_two, r.phi_two)
-
-    start_state(r.state, r.osc_own, own_rows)
+    r.filt_near[...] = r.filt_two[...]
+
+    start_state(r.state, r.osc_own, own_rows, own_rows)
 
     def own_basis(step, slot):
         kept = at(r.work, slot)
@@ -603,12 +619,9 @@
         return kept
 
     second_messages(r.acc_two, own_basis, r.plain, r.dotted, r.filt_two, r.phi_two, chunks)
-    r.put(r.acc_two)
     r.need(r.box, r.cols, r.mask_own, r.mask_ghost, r.coords_ghost)
-    geometry_by_slot(
-        r.geo, r.osc, r.coords_ghost[...], r.box[...], r.mask_ghost[...], r.wbox
-    )
-    start_state(r.state, r.osc, ghosts)
+    geometry_by_slot(r.geo, r.osc, r.coords_ghost[...], r.box[...], r.mask_ghost[...])
+    start_state(r.state, r.osc, ghosts, own_rows)
     steps(
         chunks,
         own_rows,
@@ -616,55 +629,38 @@
             at(r.at_ghost, step), r.geo, r.osc, r.state, own_rows, step, ghosts
         ),
     )
-    r.put(r.at_ghost)
     geometry_by_atom(
         r.geo_ghost,
-        r.osc,
+        r.osc_ghost,
         r.cols[...],
         ghost_lanes(r.coords_ghost),
         r.mask_ghost[...],
         r.wbox,
     )
     r.put(r.geo_ghost)
-    start_state(r.state, r.osc, own_rows)
+    r.put(r.osc_ghost)
+    start_state(r.state, r.osc_ghost, own_rows, ghosts)
     steps(
         ghost_chunks,
         ghosts,
         lambda step, slot: plain_basis(
-            at(r.a_ghost, step), r.geo_ghost, r.osc, r.state, ghosts, step, own_rows
-        ),
-    )
-    r.put(r.a_ghost)
-    r.need(r.phi_ghost, r.filt_one)
-    start_state(r.state, r.osc, own_rows)
-
-    def kept_for_back(step, slot):
-        full_basis(r.basis_ghost.at[step], r.geo_ghost, r.osc, r.state, ghosts, step)
-        phi = r.phi_ghost
-        scaled_rows(r.gs_ghost, step, step, r.filt_one, slice(0, channels), phi[:, :channels])
-        scaled_rows(
-            r.gv_ghost, step, step, r.filt_one, slice(channels, None), phi[:, channels:]
-        )
-
-    steps(ghost_chunks, ghosts, kept_for_back)
-    r.put(r.basis_ghost, r.gs_ghost, r.gv_ghost)
+            at(r.a_ghost, step), r.geo_ghost, r.osc_ghost, r.state, ghosts, step, own_rows
+        ),
+    )
 
 
 def second_ghost_kernel(sizes, chunks, ghost_chunks, r):
     own_rows = r.node.shape[0] // 2
     r.table[...] = jnp.zeros_like(r.table)
-    arrival = receive(r, r.table, sizes)
-    r.need(r.filt_two, r.acc_two)
-    arrival()
+    receive(r, r.table, sizes)
     r.put(r.table)
 
-    r.need(r.a_ghost)
     second_messages(
         r.acc_two,
         lambda step, slot: at(r.a_ghost, step),
         r.plain,
         r.dotted,
-        r.filt_two,
+        r.filt_near,
         r.table,
         ghost_chunks,
     )
@@ -676,13 +672,12 @@
     bars = jnp.concatenate([weight * slope, weight * bend * hidden[own_rows:]], 0)
     r.cot[...] = dot3(bars, r.w_hidden, nt_dims)
     r.put(r.cot)
-    r.need(r.at_ghost)
     table_cotangents(
         r.back_ghost,
         lambda step, slot: at(r.at_ghost, step),
         r.plain,
         r.dotted,
-        r.filt_two,
+        r.filt_near,
         r.cot,
         chunks,
     )
@@ -692,10 +687,10 @@
 def second_back_kernel(chunks, ghost_chunks, r):
     own_rows = r.mask_own.shape[0]
     r.need(r.box, r.cols, r.mask_own)
-    geometry_by_slot(r.geo, r.osc, r.cols[...], r.box[...], r.mask_own[...], r.wbox)
+    geometry_by_slot(r.geo, r.osc, r.cols[...], r.box[...], r.mask_own[...])
     r.need(r.cot, r.filt_two)
 
-    start_state(r.state, r.osc, own_rows)
+    start_state(r.state, r.osc, own_rows, own_rows)
 
     def slot_basis(step, slot):
         kept = at(r.work, slot)
@@ -703,23 +698,17 @@
         return kept
 
     table_cotangents(r.back, slot_basis, r.plain, r.dotted, r.filt_two, r.cot, chunks)
-    r.put(r.back)
     split_cot = at(r.work, 0)
     put_split(split_cot, 0, r.cot[...])
     r.need(r.geo_own, r.osc_own, r.phi_two)
 
-    start_state(r.state, r.osc_own, own_rows)
-
-    def own_basis(step, slot):
-        kept = r.basis.at[slot]
-        full_basis(kept, r.geo_own, r.osc_own, r.state, own_rows, step)
-        return kept
+    start_state(r.state, r.osc_own, own_rows, own_rows)
 
     second_pairs(
         r.pair,
         r.pair_own,
         split_cot,
-        own_basis,
+        lambda step: full_basis(r.geo_own, r.osc_own, r.state, own_rows, step),
         r.plain,
         r.dotted,
         r.filt_two,
@@ -727,38 +716,59 @@
         chunks,
     )
     r.put(r.pair_own)
-    r.need(r.table, r.basis_ghost)
+    r.need(r.table, r.geo_ghost, r.osc_ghost)
+    ghosts = r.table.shape[0]
+    start_state(r.state, r.osc_ghost, own_rows, ghosts)
+
 
     second_pairs(
         r.pair,
         r.pair_ghost,
         split_cot,
-        lambda step, slot: r.basis_ghost.at[step],
+        lambda step: full_basis(r.geo_ghost, r.osc_ghost, r.state, ghosts, step),
         r.plain,
         r.dotted,
         r.filt_two,
         r.table,
         ghost_chunks,
     )
-    r.put(r.pair_ghost)
-
-
-def first_back_ghost_kernel(sizes, r):
+    r.need(r.send_rows, r.w_two_out, r.inner)
+    r.send_near[...] = r.send_rows[...]
+    r.out_near[...] = r.w_two_out[...]
+    r.inner_near[...] = r.inner[...]
+
+
+def pairs_again(r, geo, osc, phi, chunks):
+    members = phi.shape[0]
+    channels = phi.shape[1] // 2
+    start_state(r.state, osc, geo.shape[1], members)
+
+    def basis_at(step):
+        return full_basis(geo, osc, r.state, members, step)
+
+    def factors_at(step, slot):
+        scaled_rows(r.gs, slot, step, r.filt_one, slice(0, channels), phi[:, :channels])
+        scaled_rows(r.gv, slot, step, r.filt_one, slice(channels, None), phi[:, channels:])
+        return at(r.gs, slot), at(r.gv, slot)
+
+    first_pairs(r.pair, r.cots, r.bars, geo, basis_at, factors_at, members, chunks)
+
+
+def first_back_ghost_kernel(sizes, chunks, r):
     own_rows = r.back.shape[0]
     channels = r.back.shape[1] // 2
-    arrival = receive(r, r.table, sizes)
-    r.need(r.send_rows, r.back)
-    arrival()
-    add_returned(r.back, r.table, r.send_rows, sizes)
-    r.need(r.w_two_out, r.inner, r.w_two_in, r.cot)
+    r.table[...] = jnp.zeros_like(r.table)
+    receive(r, r.table, sizes)
+    add_returned(r.back, r.table, r.send_near[...])
+    r.need(r.w_two_in, r.cot)
     outer = dot3(
-        jnp.concatenate([r.back[:, :channels], r.back[:, channels:]], 0), r.w_two_out, nt_dims
-    )
-    _, slope, bend = silu_parts(r.inner[:own_rows, :])
+        jnp.concatenate([r.back[:, :channels], r.back[:, channels:]], 0), r.out_near, nt_dims
+    )
+    _, slope, bend = silu_parts(r.inner_near[:own_rows, :])
     pulled = jnp.concatenate(
         [
             outer[:own_rows] * slope,
-            outer[own_rows:] * slope + outer[:own_rows] * bend * r.inner[own_rows:, :],
+            outer[own_rows:] * slope + outer[:own_rows] * bend * r.inner_near[own_rows:, :],
         ],
         0,
     )
@@ -779,19 +789,9 @@
         put_split(r.bars, (2 + i) * own_rows, both[:own_rows])
         put_split(r.bars, (5 + i) * own_rows, both[own_rows:])
     r.put(r.bars)
-    r.need(r.geo_ghost, r.gs_ghost, r.gv_ghost, r.basis_ghost)
-    first_pairs(
-        r.pair,
-        r.cots,
-        r.bars,
-        r.geo_ghost,
-        lambda step, slot: r.basis_ghost.at[step],
-        lambda step, slot: (at(r.gs_ghost, step), at(r.gv_ghost, step)),
-        r.table.shape[0],
-        r.basis_ghost.shape[0],
-    )
+    r.need(r.geo_ghost, r.osc_ghost, r.phi_ghost, r.filt_one)
+    pairs_again(r, r.geo_ghost, r.osc_ghost, r.phi_ghost, chunks)
     r.by_slot[...] = jnp.zeros_like(r.by_slot)
-    r.need(r.pair_ghost)
     members = r.table.shape[0]
     offset_gradients(r.geo_ghost, r.pair, r.pair_ghost, members, r.by_slot, r.by_atom)
     r.put(r.by_atom)
@@ -800,40 +800,24 @@
 
 def first_back_own_kernel(chunks, r):
     own_rows = r.by_atom.shape[0]
-    channels = r.phi_own.shape[1] // 2
     r.need(r.phi_own, r.filt_one, r.geo_own, r.osc_own, r.bars)
-
-    start_state(r.state, r.osc_own, own_rows)
-
-    def basis_at(step, slot):
-        kept = r.basis.at[slot]
-        full_basis(kept, r.geo_own, r.osc_own, r.state, own_rows, step)
-        return kept
-
-    def factors_at(step, slot):
-        phi, filt = r.phi_own, r.filt_one
-        scaled_rows(r.gs, slot, step, filt, slice(0, channels), phi[:, :channels])
-        scaled_rows(r.gv, slot, step, filt, slice(channels, None), phi[:, channels:])
-        return at(r.gs, slot), at(r.gv, slot)
-
-    first_pairs(r.pair, r.cots, r.bars, r.geo_own, basis_at, factors_at, own_rows, chunks)
+    pairs_again(r, r.geo_own, r.osc_own, r.phi_own, chunks)
     r.result[...] = jnp.zeros_like(r.result)
     r.need(r.pair_own, r.by_atom)
     offset_gradients(r.geo_own, r.pair, r.pair_own, own_rows, r.result, r.atoms)
     r.result[...] += (r.atoms[...] + r.by_atom[...]).T[0:8, :]
-    r.put(r.result)
+    r.need(r.send_rows)
+    r.send_near[...] = r.send_rows[...]
 
 
 def finish_kernel(sizes, r):
-    count = r.send_rows.shape[1] // 8
+    count = r.send_near.shape[1] // 8
     own_rows = r.result.shape[1]
     r.table[...] = jnp.zeros_like(r.table)
-    arrival = receive(r, r.table, sizes)
+    receive(r, r.table, sizes)
     lane = lax.broadcasted_iota(jnp.int32, (1, lanes), 1)
-    r.need(r.send_rows, r.result)
     atom = lax.broadcasted_iota(jnp.int32, (own_rows, 8 * count), 0)
-    place = jnp.where(atom == r.send_rows[...], 1.0, 0.0).astype(bf16)
-    arrival()
+    place = jnp.where(atom == r.send_near[...], 1.0, 0.0).astype(bf16)
     rows = jnp.zeros((8, lanes), f32)
     for number in range(8):
         shift = ((2 * number - 7) * count) % lanes
@@ -873,9 +857,15 @@
     return value if isinstance(value, tuple) else (value,)
 
 
+def flat(entry):
+    if isinstance(entry, list):
+        return entry
+    return [(entry[0], kind) for kind in as_tuple(entry[1])]
+
+
 class Slot:
     def __init__(self, name, value):
-        self.name, self.arrays = name, as_tuple(value)
+        self.name, self.arrays, self.near = name, as_tuple(value), False
 
 
 class Slots:
@@ -883,7 +873,10 @@
         object.__setattr__(self, name, Slot(name, value))
 
 
-def call(kernel, v, loads, outs, scratch, index=(), raw=(), scalars=(), sent=()):
+def call(kernel, v, loads, outs, scratch, index=(), raw=(), scalars=(), sent=(), near=None):
+    near = near or dict()
+    raw = raw + tuple(slot for slot in loads if slot.near)
+    loads = tuple(slot for slot in loads if not slot.near)
     args, kinds, shapes, buffers = [], [], [], []
     copied = [(slot, pltpu.VMEM) for slot in loads] + [(slot, pltpu.SMEM) for slot in index]
     copies = 0
@@ -894,17 +887,24 @@
             buffers.append(space(array.shape, array.dtype))
             copies += 1
     for slot in raw + scalars:
-        args.append(slot.arrays[0])
-        kinds.append(pl.BlockSpec(memory_space=pl.ANY if slot in raw else pltpu.SMEM))
+        for array in slot.arrays:
+            args.append(array)
+            kinds.append(pl.BlockSpec(memory_space=pltpu.VMEM if slot in raw else pltpu.SMEM))
     for shape, types in outs.values():
         for kind in as_tuple(types):
             shapes.append(pltpu.HBM(shape, kind))
             buffers.append(pltpu.VMEM(shape, kind))
             copies += 1
+    places = [pltpu.HBM] * len(shapes)
+    for entry in near.values():
+        for shape, kind in flat(entry):
+            shapes.append(jax.ShapeDtypeStruct(shape, kind))
+            places.append(pltpu.VMEM)
     if sent:
         shapes.append(pltpu.HBM(sent, f32))
-    for shape, types in scratch.values():
-        for kind in as_tuple(types):
+        places.append(pltpu.HBM)
+    for entry in scratch.values():
+        for shape, kind in flat(entry):
             buffers.append(pltpu.VMEM(shape, kind))
     buffers.append(pltpu.SemaphoreType.DMA((copies + 1,)))
     buffers.append(pltpu.SemaphoreType.DMA((8,)))
@@ -932,17 +932,21 @@
                 copy.start()
                 r.loads[key].append(copy)
         for slot in raw + scalars:
-            setattr(r, slot.name, ins.pop(0))
+            group = tuple(ins.pop(0) for _ in slot.arrays)
+            setattr(r, slot.name, group if len(group) > 1 else group[0])
         for name, (shape, types) in outs.items():
             group, key = taken(name, len(as_tuple(types)))
             r.stores[key] = []
             for buffer in group:
                 copy = pltpu.make_async_copy(buffer, targets.pop(0), sems.pop(0))
                 r.stores[key].append(copy)
+        for name, entry in near.items():
+            group = tuple(targets.pop(0) for _ in flat(entry))
+            setattr(r, name, group if len(group) > 1 else group[0])
         if sent:
             r.out = targets.pop(0)
-        for name, (shape, types) in scratch.items():
-            taken(name, len(as_tuple(types)))
+        for name, entry in scratch.items():
+            taken(name, len(flat(entry)))
         kernel(r)
         r.close()
 
@@ -950,15 +954,18 @@
         run,
         out_shape=shapes,
         in_specs=kinds,
-        out_specs=[pl.BlockSpec(memory_space=pltpu.HBM) for _ in shapes],
+        out_specs=[pl.BlockSpec(memory_space=place) for place in places],
         scratch_shapes=buffers,
-        compiler_params=pltpu.CompilerParams(vmem_limit_bytes=48 * 1024 * 1024),
+        compiler_params=pltpu.CompilerParams(vmem_limit_bytes=20 * 1024 * 1024),
         name=kernel.func.__name__,
     )(*args)
     results = list(results)
     for name, (shape, types) in outs.items():
         group = tuple(results.pop(0) for _ in as_tuple(types))
         setattr(v, name, group)
+    for name, entry in near.items():
+        setattr(v, name, tuple(results.pop(0) for _ in flat(entry)))
+        getattr(v, name).near = True
     if sent:
         v.arrived = exchanged(results.pop(0))
 
@@ -1005,10 +1012,10 @@
     def factors(chunks):
         return ((chunks, wide, channels), pair)
 
-    geometry = ((geo_slots, n, wide), f32)
-    osc = ((osc_slots, n, wide), f32)
-    state = ((2, n, wide), f32)
-    wbox = ((n, wide), f32)
+    geometry = ((geo_slots, n, lanes), f32)
+    osc = ((osc_slots, n, lanes), f32)
+    state = [((2, n, wide), f32), ((2, n, lanes), f32)]
+    wbox = ((n, lanes), f32)
     pairs = ((8, n, wide), f32)
     cots = ((2, 8 * n, wide), f32)
 
@@ -1020,10 +1027,10 @@
         dict(
             box=((n, n), f32),
             table=((n, channels + lanes), f32),
-            stage=((ghosts, channels + lanes), f32),
+            stage=((8, 1, count * channels + lanes), f32),
         ),
         index=(v.send_rows,),
-        sent=(devices, count, channels + lanes),
+        sent=(devices, 1, count * channels + lanes),
     )
     call(
         part(first_own_kernel, scale, own_chunks),
@@ -1036,7 +1043,6 @@
             mask_ghost=((ghosts, n), f32),
             filt_one=((orders, 2 * channels), f32),
             filt_two=((orders, channels), f32),
-            acc=((8 * n, channels), f32),
             geo_own=geometry,
             osc_own=osc,
             phi_own=((n, 2 * channels), f32),
@@ -1048,11 +1054,19 @@
             state=state,
             work=((2, 8 * n, wide), pair),
         ),
+        near=dict(
+            acc=((8 * n, channels), f32),
+            cols_near=((n, n), f32),
+            mask_near=((ghosts, n), f32),
+            filt_near=((orders, 2 * channels), f32),
+            in_near=((channels, channels), f32),
+            out_near=((channels, 2 * channels), f32),
+        ),
     )
     call(
         part(first_ghost_kernel, sizes, ghost_chunks),
         v,
-        (v.w_one_in, v.cols, v.mask_ghost, v.w_one_out, v.filt_one, v.acc, v.w_left, v.w_right, v.embedding, v.w_two_in, v.w_two_out),
+        (v.cols_near, v.mask_near, v.filt_near, v.in_near, v.out_near, v.acc, v.w_left, v.w_right, v.embedding, v.w_two_in, v.w_two_out),
         dict(
             node=((2 * n, channels), f32),
             inner=((2 * n, channels), f32),
@@ -1079,15 +1093,10 @@
     call(
         part(second_own_kernel, own_chunks, ghost_chunks),
         v,
-        (v.geo_own, v.osc_own, v.phi_two, v.filt_two, v.box, v.cols, v.mask_own, v.mask_ghost, v.coords_ghost, v.phi_ghost, v.filt_one),
-        dict(
-            acc_two=((2 * n, channels), f32),
-            at_ghost=((own_chunks, 2 * ghosts, wide), pair),
+        (v.geo_own, v.osc_own, v.phi_two, v.filt_two, v.box, v.cols, v.mask_own, v.mask_ghost, v.coords_ghost),
+        dict(
             geo_ghost=geometry,
-            a_ghost=((ghost_chunks, 2 * n, wide), pair),
-            basis_ghost=((ghost_chunks, 3, n, wide), f32),
-            gs_ghost=factors(ghost_chunks),
-            gv_ghost=factors(ghost_chunks),
+            osc_ghost=osc,
         ),
         dict(
             geo=geometry,
@@ -1098,11 +1107,17 @@
             plain=factors(2),
             dotted=factors(2),
         ),
+        near=dict(
+            acc_two=((2 * n, channels), f32),
+            at_ghost=((own_chunks, 2 * ghosts, wide), pair),
+            a_ghost=((ghost_chunks, 2 * n, wide), pair),
+            filt_near=((orders, channels), f32),
+        ),
     )
     call(
         part(second_ghost_kernel, sizes, own_chunks, ghost_chunks),
         v,
-        (v.filt_two, v.acc_two, v.a_ghost, v.node, v.w_hidden, v.w_energy, v.at_ghost),
+        (v.filt_near, v.acc_two, v.a_ghost, v.node, v.w_hidden, v.w_energy, v.at_ghost),
         dict(
             cot=((2 * n, channels), f32),
             table=((ghosts, 2 * channels), f32),
@@ -1119,14 +1134,11 @@
     call(
         part(second_back_kernel, own_chunks, ghost_chunks),
         v,
-        (v.box, v.cols, v.mask_own, v.cot, v.filt_two, v.geo_own, v.osc_own, v.phi_two, v.table, v.basis_ghost),
-        dict(
-            back=((n, 2 * channels), f32),
+        (v.box, v.cols, v.mask_own, v.cot, v.filt_two, v.geo_own, v.osc_own, v.phi_two, v.table, v.geo_ghost, v.osc_ghost, v.send_rows, v.w_two_out, v.inner),
+        dict(
             pair_own=((2, n, lanes), f32),
-            pair_ghost=((2, n, lanes), f32),
-        ),
-        dict(
-            basis=((2, 3, n, wide), f32),
+        ),
+        dict(
             geo=geometry,
             osc=osc,
             state=state,
@@ -1136,11 +1148,18 @@
             dotted=factors(2),
             pair=((2, n, wide), f32),
         ),
+        near=dict(
+            back=((n, 2 * channels), f32),
+            pair_ghost=((2, n, lanes), f32),
+            send_near=((1, ghosts), jnp.int32),
+            out_near=((channels, channels), f32),
+            inner_near=((2 * n, channels), f32),
+        ),
     )
     call(
-        part(first_back_ghost_kernel, sizes),
+        part(first_back_ghost_kernel, sizes, ghost_chunks),
         v,
-        (v.back, v.w_two_out, v.inner, v.w_two_in, v.cot, v.maps, v.w_left, v.w_right, v.geo_ghost, v.gs_ghost, v.gv_ghost, v.basis_ghost, v.pair_ghost),
+        (v.send_near, v.back, v.out_near, v.inner_near, v.w_two_in, v.cot, v.maps, v.w_left, v.w_right, v.phi_ghost, v.filt_one, v.osc_ghost, v.geo_ghost, v.pair_ghost),
         dict(
             bars=((8 * n, channels), pair),
             by_atom=((n, lanes), f32),
@@ -1150,16 +1169,18 @@
             by_slot=((8, lanes), f32),
             pair=pairs,
             cots=cots,
-        ),
-        index=(v.send_rows,),
+            state=state,
+            gs=factors(2),
+            gv=factors(2),
+        ),
         raw=(v.arrived,),
         sent=(devices, 8, lanes),
     )
     call(
         part(first_back_own_kernel, own_chunks),
         v,
-        (v.phi_own, v.filt_one, v.geo_own, v.osc_own, v.bars, v.pair_own, v.by_atom),
-        dict(result=((8, lanes), f32)),
+        (v.phi_own, v.filt_one, v.geo_own, v.osc_own, v.bars, v.pair_own, v.by_atom, v.send_rows),
+        dict(),
         dict(
             atoms=((n, lanes), f32),
             pair=pairs,
@@ -1167,13 +1188,13 @@
             state=state,
             gs=factors(2),
             gv=factors(2),
-            basis=((2, 3, n, wide), f32),
-        ),
+        ),
+        near=dict(result=((8, lanes), f32), send_near=((1, ghosts), jnp.int32)),
     )
     call(
         part(finish_kernel, sizes),
         v,
-        (v.send_rows, v.result),
+        (v.send_near, v.result),
         dict(forces=((3, n), f32), product=((3, n), f32)),
         dict(table=((64, lanes), f32)),
         raw=(v.arrived,),

time: 98.1 us -> 91.1 us (0.929)
  Pallas kernels: 65 us -> 56.5 us
  waiting for transfers between devices: 13 us -> 14.4 us
    pallas_call x9, Pallas kernels: 65 us -> 56.5 us  [call(): pl.pallas_call(run, out_shape=shapes, in_specs=kinds, out_specs=[pl.Block...]
    all_to_all x4, waiting for transfers between devices: 13 us -> 14.4 us  [exchanged(): return lax.all_to_all(buffer, ('bx', 'by'), 0, 0)]
  transfers between devices with their start and end apart: 4 -> 4, of which waited for: 3 -> 3; matrix products, arithmetic and copies ran while one was open for 0% -> 0% of each run, Pallas kernels for 40% -> 38%
where the time goes in v1:
time: 91.1 us; the launch traced here: 89.4 us
  Pallas kernels  56.5 us (62%)
  starting transfers between devices  17 us (19%)
  waiting for transfers between devices  14.4 us (16%)
  between operations  1.54 us (2%)
    pallas_call x9, Pallas kernels, call(): pl.pallas_call(run, out_shape=shapes, in_specs=kinds, out_specs=[pl.Block...  56.5 us
    all_to_all x4, starting transfers between devices, exchanged(): return lax.all_to_all(buffer, ('bx', 'by'), 0, 0)  17 us
    all_to_all x4, waiting for transfers between devices, exchanged(): return lax.all_to_all(buffer, ('bx', 'by'), 0, 0)  14.4 us
  transfers between devices with their start and end apart: 4, of which 3 were waited for; matrix products, arithmetic and copies ran while one was open for 0% of the time, Pallas kernels for 38%

profile of v1, /device:TPU:4, one launch (start us, length us, event | category | flops | bytes accessed | tf_op | source)
XLA Modules:
  0.0 89.4 jit_solution(7543502080656852544)
XLA Ops:
  0.6 1.9 %pack_kernel.1 = f32[32,1,2176]{2,1,0:T(1,128)} custom-call(f32[3,128]{1,0:T(4,128)} %refs_0_.5, f32[3,128]{1,0:T(4,128)} %refs_1_.5, f32[128,256]{1,0:T(8,128)} %refs_2_.5, s32[1,64]{1,0:T(1,128)} %refs_8_.1), custom_call_target="tpu_custom_call" | custom-call | tf_op jit(solution)/shard_map/pack_kernel/pallas_call | solution.py:953
  2.5 6.1 %all-to-all-start = ((f32[32,1,2176]{2,1,0:T(1,128)}), f32[32,1,2176]{2,1,0:T(1,128)S(1)}, u32[]{:S(2)}, u32[]{:S(2)}) async-start(f32[32,1,2176]{2,1,0:T(1,128)} %pack_kernel.1), calls=%async_computation | async-start | bytes 557056 | tf_op jit(solution)/shard_map/all_to_all | solution.py:974
  8.6 7.9 %first_own_kernel.1 = (f32[128,128]{1,0:T(8,128)}, f32[128,128]{1,0:T(8,128)}, f32[128,128]{1,0:T(8,128)}, f32[64,128]{1,0:T(8,128)}, f32[20,512]{1,0:T(8,128)},...) custom-call(f32[3,128]{1,0:T(4,128)} %refs_0_.5, ...), custom_call_target="tpu_custom_call" | custom-call | tf_op jit(solution)/shard_map/first_own_kernel/pallas_call | solution.py:953
  16.5 2.2 %all-to-all-done.refs_6_ = f32[32,1,2176]{2,1,0:T(1,128)S(1)} async-done(((f32[32,1,2176]{2,1,0:T(1,128)}), f32[32,1,2176]{2,1,0:T(1,128)S(1)}, u32[]{:S(2)}, u32[]{:S(2)}) %all-to-all-start) | async-done | bytes 278560 | tf_op jit(solution)/shard_map/all_to_all | solution.py:974
  18.7 7.8 %first_ghost_kernel.1 = (f32[256,256]{1,0:T(8,128)}, f32[256,256]{1,0:T(8,128)}, f32[1536,256]{1,0:T(8,128)}, f32[128,512]{1,0:T(8,128)}, f32[64,512]{1,0:T(8,12...) custom-call(f32[256,256]{1,0:T(8,128)} %refs_3_.7, f32[256,256]{1,0:T(8,128)} %refs_4_.5, f32[128,256]{1,0:T(8,128)} %refs_2_.5, ...), custom_call_target="tpu_custom_call" | custom-call | tf_op jit(solution)/shard_map/first_ghost_kernel/pallas_call | solution.py:953
  26.4 3.6 %all-to-all-start.1 = ((f32[32,8,512]{2,1,0:T(8,128)}), f32[32,8,512]{2,1,0:T(8,128)S(1)}, u32[]{:S(2)}, u32[]{:S(2)}) async-start(f32[32,8,512]{2,1,0:T(8,128)} %get-tuple-element.54), calls=%async_computation.1 | async-start | bytes 1048576 | tf_op jit(solution)/shard_map/all_to_all | solution.py:974
  30.7 6.8 %second_own_kernel.1 = (f32[8,128,128]{2,1,0:T(8,128)}, f32[5,128,128]{2,1,0:T(8,128)}, f32[256,256]{1,0:T(8,128)S(1)}, bf16[10,128,256]{2,1,0:T(8,128)(2,1)S(1)...) custom-call(f32[8,128,128]{2,1,0:T(8,128)} %get-tuple-element.55.ref, ...), custom_call_target="tpu_custom_call" | custom-call | tf_op jit(solution)/shard_map/second_own_kernel/pallas_call | solution.py:953
  37.5 7.5 %all-to-all-done.1.refs_3_ = f32[32,8,512]{2,1,0:T(8,128)S(1)} async-done(((f32[32,8,512]{2,1,0:T(8,128)}), f32[32,8,512]{2,1,0:T(8,128)S(1)}, u32[]{:S(2)}, u32[]{:S(2)}) %all-to-all-start.1) | async-done | bytes 524320 | tf_op jit(solution)/shard_map/all_to_all | solution.py:974
  45.1 5.0 %second_ghost_kernel.1 = (f32[256,256]{1,0:T(8,128)}, f32[64,512]{1,0:T(8,128)}, f32[32,8,512]{2,1,0:T(8,128)}) custom-call(f32[256,256]{1,0:T(8,128)} %get-tuple-element.53.refs_0_, f32[256,256]{1,0:T(8,128)} %refs_1_.7, f32[1,256]{1,0:T(1,128)} %bitcast.1, f32[32,8,512]{2,1,0:T(8,128)S(1)} %all-to-all-done.1.refs_3_, ...), custom_call_target="tpu_custom_call" | custom-call | tf_op jit(solution)/shard_map/second_ghost_kernel/pallas_call | solution.py:953
  50.1 3.6 %all-to-all-start.2 = ((f32[32,8,512]{2,1,0:T(8,128)}), f32[32,8,512]{2,1,0:T(8,128)S(1)}, u32[]{:S(2)}, u32[]{:S(2)}) async-start(f32[32,8,512]{2,1,0:T(8,128)} %get-tuple-element.76), calls=%async_computation.2 | async-start | bytes 1048576 | tf_op jit(solution)/shard_map/all_to_all | solution.py:974
  53.7 10.3 %second_back_kernel.1 = (f32[2,128,128]{2,1,0:T(8,128)}, f32[128,512]{1,0:T(8,128)S(1)}, f32[2,128,128]{2,1,0:T(8,128)S(1)}, s32[1,64]{1,0:T(1,128)S(1)}, f32[25...) custom-call(f32[128,128]{1,0:T(8,128)} %get-tuple-element.59.refs_4_.refs_0_, f32[128,128]{1,0:T(8,128)} %get-tuple-element.60.refs_5_.refs_1_, ...), custom_call_target="tpu_custom_call" | custom-call | tf_op jit(solution)/shard_map/second_back_kernel/pallas_call | solution.py:953
  64.1 4.7 %all-to-all-done.2.refs_9_ = f32[32,8,512]{2,1,0:T(8,128)S(1)} async-done(((f32[32,8,512]{2,1,0:T(8,128)}), f32[32,8,512]{2,1,0:T(8,128)S(1)}, u32[]{:S(2)}, u32[]{:S(2)}) %all-to-all-start.2) | async-done | bytes 524320 | tf_op jit(solution)/shard_map/all_to_all | solution.py:974
  68.7 7.2 %first_back_ghost_kernel.1 = (bf16[1024,256]{1,0:T(8,128)(2,1)}, bf16[1024,256]{1,0:T(8,128)(2,1)}, f32[128,128]{1,0:T(8,128)}, f32[32,8,128]{2,1,0:T(8,128)}) custom-call(f32[256,256]{1,0:T(8,128)} %refs_0_.7, f32[256,256]{1,0:T(8,128)} %get-tuple-element.70.refs_3_.refs_1_, f32[1536,256]{1,0:T(8,128)} %get-tuple-element.71.refs_2_, f32[256,256]{1,0:T(8,128)} %refs_3_.7, ...), custom_call_target="tpu_custom_call" | custom-call | tf_op jit(solution)/shard_map/first_back_ghost_kernel/pallas_call | solution.py:953
  75.9 3.6 %all-to-all-start.3 = ((f32[32,8,128]{2,1,0:T(8,128)}), f32[32,8,128]{2,1,0:T(8,128)S(1)}, u32[]{:S(2)}, u32[]{:S(2)}) async-start(f32[32,8,128]{2,1,0:T(8,128)} %get-tuple-element.84), calls=%async_computation.3 | async-start | bytes 262144 | tf_op jit(solution)/shard_map/all_to_all | solution.py:974
  79.5 8.8 %first_back_own_kernel.1 = (f32[8,128]{1,0:T(8,128)S(1)}, s32[1,64]{1,0:T(1,128)S(1)}) custom-call(f32[128,512]{1,0:T(8,128)} %get-tuple-element.85.refs_0_, f32[20,512]{1,0:T(8,128)} %get-tuple-element.73.refs_6_.refs_1_, f32[8,128,128]{2,1,0:T(8,128)} %get-tuple-element.55.refs_0_.refs_5_.refs_2_, ...), custom_call_target="tpu_custom_call" | custom-call | tf_op jit(solution)/shard_map/first_back_own_kernel/pallas_call | solution.py:953
  88.3 0.0 all-to-all-done.3.refs_0_
  88.3 1.0 %finish_kernel.1 = (f32[3,128]{1,0:T(4,128)}, f32[3,128]{1,0:T(4,128)}) custom-call(f32[32,8,128]{2,1,0:T(8,128)S(1)} %all-to-all-done.3.refs_0_, s32[1,64]{1,0:T(1,128)S(1)} %get-tuple-element.90.refs_1_, f32[8,128]{1,0:T(8,128)S(1)} %get-tuple-element.91.refs_2_), custom_call_target="tpu_custom_call" | custom-call | tf_op jit(solution)/shard_map/finish_kernel/pallas_call | solution.py:953
Async XLA Ops:
  2.5 16.2 %all-to-all-start = ((f32[32,1,2176]{2,1,0:T(1,128)}), f32[32,1,2176]{2,1,0:T(1,128)S(1)}, u32[]{:S(2)}, u32[]{:S(2)}) async-start(f32[32,1,2176]{2,1,0:T(1,128)} %pack_kernel.1), calls=%async_computation | async-start | bytes 557056 | tf_op jit(solution)/shard_map/all_to_all | solution.py:974
  26.4 18.7 %all-to-all-start.1 = ((f32[32,8,512]{2,1,0:T(8,128)}), f32[32,8,512]{2,1,0:T(8,128)S(1)}, u32[]{:S(2)}, u32[]{:S(2)}) async-start(f32[32,8,512]{2,1,0:T(8,128)} %get-tuple-element.54), calls=%async_computation.1 | async-start | bytes 1048576 | tf_op jit(solution)/shard_map/all_to_all | solution.py:974
  50.1 18.6 %all-to-all-start.2 = ((f32[32,8,512]{2,1,0:T(8,128)}), f32[32,8,512]{2,1,0:T(8,128)S(1)}, u32[]{:S(2)}, u32[]{:S(2)}) async-start(f32[32,8,512]{2,1,0:T(8,128)} %get-tuple-element.76), calls=%async_computation.2 | async-start | bytes 1048576 | tf_op jit(solution)/shard_map/all_to_all | solution.py:974
  75.9 12.4 %all-to-all-start.3 = ((f32[32,8,128]{2,1,0:T(8,128)}), f32[32,8,128]{2,1,0:T(8,128)S(1)}, u32[]{:S(2)}, u32[]{:S(2)}) async-start(f32[32,8,128]{2,1,0:T(8,128)} %get-tuple-element.84), calls=%async_computation.3 | async-start | bytes 262144 | tf_op jit(solution)/shard_map/all_to_all | solution.py:974

commit v2 on v1

--- a/solution.py
+++ b/solution.py
@@ -168,10 +168,12 @@
     return jnp.where(found, 1.0, 0.0).astype(f32)
 
 
-def geometry_by_atom(geo, osc, columns, table, mask, wbox):
-    repeats = lanes // mask.shape[0]
-    table = jnp.concatenate([table] * repeats, 1)
-    wbox[...] = jnp.concatenate([mask] * repeats, 0).T
+def fill_mask(wbox, mask):
+    wbox[...] = jnp.concatenate([mask] * (lanes // mask.shape[0]), 0).T
+
+
+def geometry_by_atom(geo, osc, columns, table, wbox):
+    table = jnp.concatenate([table] * (lanes // table.shape[1]), 1)
     fill_geometry(
         geo,
         osc,
@@ -180,6 +182,12 @@
         lambda start: wbox[start : start + row_block, :],
         geo.shape[1],
     )
+
+
+def picked(place, value):
+    high, low = split(value)
+    rest = (value - high.astype(f32) - low.astype(f32)).astype(bf16)
+    return mxu(place, high) + mxu(place, low) + mxu(place, rest)
 
 
 def geometry_by_slot(geo, osc, columns, centre, mask):
@@ -491,19 +499,19 @@
 
 def first_own_kernel(scale, chunks, r):
     own_rows = r.positions.shape[1]
+    ghosts = r.mask_ghost.shape[0]
     r.box[...] = jnp.zeros_like(r.box)
     r.need(r.positions, r.tangent, r.neighbours)
     r.box[0:3, :] = r.positions[...]
     r.box[3:6, :] = r.tangent[...]
     r.cols[...] = r.box[...].T
     r.mask_own[...] = listed(r.neighbours, 0, own_rows)
-    r.mask_ghost[...] = listed(r.neighbours, own_rows, r.mask_ghost.shape[0])
+    r.mask_ghost[...] = listed(r.neighbours, own_rows, ghosts)
     r.put(r.box, r.cols, r.mask_own, r.mask_ghost)
-    r.cols_near[...] = r.cols[...]
-    r.mask_near[...] = r.mask_ghost[...]
-    geometry_by_atom(r.geo_own, r.osc_own, r.cols[...], r.box[...], r.mask_own[...], r.wbox)
+    fill_mask(r.wbox, r.mask_own[...])
+    geometry_by_atom(r.geo_own, r.osc_own, r.cols[...], r.box[...], r.wbox)
     r.put(r.geo_own, r.osc_own)
-    r.need(r.w_one_in, r.w_one_out, r.embedding, r.filter_one, r.filter_two)
+    r.need(r.w_one_in, r.w_one_out, r.embedding, r.filter_one, r.filter_two, r.send_rows)
     r.filt_one[...] = r.filter_one[...] * scale
     r.filt_two[...] = r.filter_two[...] * scale
     r.put(r.filt_one, r.filt_two)
@@ -526,13 +534,49 @@
         own_rows,
         chunks,
     )
-
-
-def first_ghost_kernel(sizes, chunks, r):
-    own_rows = r.embedding.shape[0]
-    channels = r.embedding.shape[1]
+    r.put(r.acc)
+    sent = jnp.concatenate([r.send_rows[...]] * (own_rows // ghosts), 1)
+    atom = lax.broadcasted_iota(jnp.int32, (own_rows, own_rows), 0)
+    place = jnp.where(atom == sent, 1.0, 0.0).astype(f32).T[:ghosts].astype(bf16)
+    r.cols_sent[...] = picked(place, r.cols[...])
+    r.emb_sent[...] = picked(place, r.embedding[...])
+    fill_mask(r.wbox, r.mask_ghost[...])
+    r.wbox_sent[...] = mxu(place, r.wbox[...].astype(bf16))
+    for i in range(8):
+        r.acc_sent[i * ghosts : (i + 1) * ghosts, :] = picked(
+            place, r.acc[i * own_rows : (i + 1) * own_rows, :]
+        )
+
+
+def node_states(acc, embedding, maps, node, inner, w_left, w_right, w_two_in, w_two_out):
+    rows = embedding.shape[0]
+    top = 2 * rows
+    half = 3 * rows
+    ah, al = split(acc[top:, :])
+    maps[0 : 2 * half, :] = three(ah, al, *split(w_left[...]))
+    maps[2 * half :, :] = three(ah, al, *split(w_right[...]))
+    total = embedding[...] + acc[0:rows, :]
+    moved = acc[rows:top, :]
+    for i in range(3):
+        a, b = i * rows, (i + 1) * rows
+        left, left_dot = maps[a:b, :], maps[half + a : half + b, :]
+        right = maps[2 * half + a : 2 * half + b, :]
+        right_dot = maps[3 * half + a : 3 * half + b, :]
+        total = total + left * right
+        moved = moved + left_dot * right + left * right_dot
+    node[0:rows, :] = total
+    node[rows:, :] = moved
+    inner[...] = dot3(node[...], w_two_in)
+    value, slope, _ = silu_parts(inner[0:rows, :])
+    outer = dot3(jnp.concatenate([value, slope * inner[rows:, :]], 0), w_two_out)
+    return outer[:rows], outer[rows:]
+
+
+def first_sent_kernel(sizes, chunks, r):
+    channels = r.emb_sent.shape[1]
     r.table[...] = jnp.zeros_like(r.table)
-    count = r.table.shape[0] // 8
+    members = r.table.shape[0]
+    count = members // 8
     gap = lanes // count
     for number, target in enumerate(offsets):
         device, inside = neighbour_id(target, sizes)
@@ -552,12 +596,11 @@
         silu_parts(dot3(r.table[:, :channels], r.in_near))[0], r.out_near
     )
     r.put(r.phi_ghost)
-    members = r.mask_near.shape[0]
     geometry_by_atom(
-        r.geo, r.osc, r.cols_near[...], ghost_lanes(r.coords_ghost), r.mask_near[...], r.wbox
+        r.geo, r.osc, r.cols_sent[...], ghost_lanes(r.coords_ghost), r.wbox_sent
     )
     first_messages(
-        r.acc,
+        r.acc_sent,
         r.geo,
         r.osc,
         r.state,
@@ -569,34 +612,21 @@
         members,
         chunks,
     )
-    r.need(r.w_left, r.w_right, r.embedding, r.w_two_in, r.w_two_out, r.send_rows)
-    top = 2 * own_rows
-    half = 3 * own_rows
-    acc, maps = r.acc, r.maps
-    ah, al = split(acc[top:, :])
-    maps[0 : 2 * half, :] = three(ah, al, *split(r.w_left[...]))
-    maps[2 * half :, :] = three(ah, al, *split(r.w_right[...]))
-    r.put(r.maps)
-    total = r.embedding[...] + acc[0:own_rows, :]
-    moved = acc[own_rows:top, :]
-    for i in range(3):
-        a, b = i * own_rows, (i + 1) * own_rows
-        left, left_dot = maps[a:b, :], maps[half + a : half + b, :]
-        right = maps[2 * half + a : 2 * half + b, :]
-        right_dot = maps[3 * half + a : 3 * half + b, :]
-        total = total + left * right
-        moved = moved + left_dot * right + left * right_dot
-    r.node[0:own_rows, :] = total
-    r.node[own_rows:, :] = moved
-    r.put(r.node)
-    r.inner[...] = dot3(r.node[...], r.w_two_in)
-    r.put(r.inner)
-    value, slope, _ = silu_parts(r.inner[0:own_rows, :])
-    outer = dot3(jnp.concatenate([value, slope * r.inner[own_rows:, :]], 0), r.w_two_out)
-    r.phi_two[:, :channels] = outer[:own_rows]
-    r.phi_two[:, channels:] = outer[own_rows:]
-    r.put(r.phi_two)
-    send_gathered(r, r.phi_two, r.stage, r.send_rows, sizes)
+    r.need(r.w_left, r.w_right, r.w_two_in, r.w_two_out)
+    plain, dotted = node_states(
+        r.acc_sent,
+        r.emb_sent,
+        r.maps,
+        r.node,
+        r.inner,
+        r.w_left,
+        r.w_right,
+        r.w_two_in,
+        r.w_two_out,
+    )
+    r.stage[:, :channels] = plain
+    r.stage[:, channels:] = dotted
+    send_groups(r, r.stage, sizes)
 
 
 def ghost_lanes(coords):
@@ -607,10 +637,45 @@
 def second_own_kernel(chunks, ghost_chunks, r):
     own_rows = r.mask_own.shape[0]
     ghosts = r.mask_ghost.shape[0]
+    channels = r.embedding.shape[1]
+    r.need(r.cols, r.mask_ghost, r.coords_ghost)
+    fill_mask(r.wbox, r.mask_ghost[...])
+    geometry_by_atom(
+        r.geo_ghost, r.osc_ghost, r.cols[...], ghost_lanes(r.coords_ghost), r.wbox
+    )
+    r.put(r.geo_ghost, r.osc_ghost)
+    r.need(r.phi_ghost, r.filt_one, r.acc)
+    first_messages(
+        r.acc,
+        r.geo_ghost,
+        r.osc_ghost,
+        r.state,
+        r.work_one,
+        r.gs,
+        r.gv,
+        r.phi_ghost,
+        r.filt_one,
+        ghosts,
+        ghost_chunks,
+    )
+    r.need(r.w_left, r.w_right, r.w_two_in, r.w_two_out, r.embedding)
+    plain, dotted = node_states(
+        r.acc,
+        r.embedding,
+        r.maps,
+        r.node,
+        r.inner,
+        r.w_left,
+        r.w_right,
+        r.w_two_in,
+        r.w_two_out,
+    )
+    r.phi_two[:, :channels] = plain
+    r.phi_two[:, channels:] = dotted
+    r.put(r.node, r.maps, r.inner, r.phi_two)
     r.acc_two[...] = jnp.zeros_like(r.acc_two)
-    r.need(r.geo_own, r.osc_own, r.filt_two, r.phi_two)
+    r.need(r.geo_own, r.osc_own, r.filt_two)
     r.filt_near[...] = r.filt_two[...]
-
     start_state(r.state, r.osc_own, own_rows, own_rows)
 
     def own_basis(step, slot):
@@ -618,27 +683,22 @@
         plain_basis(kept, r.geo_own, r.osc_own, r.state, own_rows, step, own_rows)
         return kept
 
-    second_messages(r.acc_two, own_basis, r.plain, r.dotted, r.filt_two, r.phi_two, chunks)
-    r.need(r.box, r.cols, r.mask_own, r.mask_ghost, r.coords_ghost)
+    second_messages(r.acc_two, own_basis, r.gs, r.gv, r.filt_two, r.phi_two, chunks)
+    r.need(r.box)
     geometry_by_slot(r.geo, r.osc, r.coords_ghost[...], r.box[...], r.mask_ghost[...])
     start_state(r.state, r.osc, ghosts, own_rows)
-    steps(
-        chunks,
-        own_rows,
-        lambda step, slot: plain_basis(
-            at(r.at_ghost, step), r.geo, r.osc, r.state, own_rows, step, ghosts
-        ),
-    )
-    geometry_by_atom(
-        r.geo_ghost,
-        r.osc_ghost,
-        r.cols[...],
-        ghost_lanes(r.coords_ghost),
-        r.mask_ghost[...],
-        r.wbox,
-    )
-    r.put(r.geo_ghost)
-    r.put(r.osc_ghost)
+
+    def slot_rows(step, slot):
+        kept = at(r.work, slot)
+        plain_basis(kept, r.geo, r.osc, r.state, own_rows, step, ghosts)
+        for i in range(wide // lanes):
+            part = slice(i * lanes, (i + 1) * lanes)
+            order = step * (wide // lanes) + i
+            for half, place in zip(kept, (slice(0, lanes), slice(lanes, wide))):
+                r.at_plain[order, :, place] = half[0:ghosts, part]
+                r.at_dot[order, :, place] = half[ghosts : 2 * ghosts, part]
+
+    steps(chunks, own_rows, slot_rows)
     start_state(r.state, r.osc_ghost, own_rows, ghosts)
     steps(
         ghost_chunks,
@@ -649,7 +709,33 @@
     )
 
 
-def second_ghost_kernel(sizes, chunks, ghost_chunks, r):
+def ghost_cotangents(back, plain, dotted, filt, cot):
+    orders, height, _ = plain.shape
+    own_rows = cot.shape[0] // 2
+    channels = cot.shape[1]
+    beside = jnp.concatenate([cot[0:own_rows, :], cot[own_rows:, :]], 1)
+    high, low = split(beside)
+    both = jnp.concatenate([high, high], 0)
+    rest = jnp.concatenate([low, jnp.zeros_like(low)], 0)
+    together = orders // 4
+    value = jnp.zeros((height, channels), f32)
+    moved = jnp.zeros((height, channels), f32)
+    for start in range(0, orders, together):
+        rows = plain[start : start + together].reshape(together * height, wide)
+        first = mxu(rows, both) + mxu(rows, rest)
+        rows = dotted[start : start + together].reshape(together * height, wide)
+        second = first[:, channels:] + (
+            mxu(rows, both[:, :channels]) + mxu(rows, rest[:, :channels])
+        )
+        for i in range(together):
+            weight = filt[start + i : start + i + 1, :]
+            value = value + weight * first[i * height : (i + 1) * height, :channels]
+            moved = moved + weight * second[i * height : (i + 1) * height, :]
+    back[:, :channels] = value
+    back[:, channels:] = moved
+
+
+def second_ghost_kernel(sizes, ghost_chunks, r):
     own_rows = r.node.shape[0] // 2
     r.table[...] = jnp.zeros_like(r.table)
     receive(r, r.table, sizes)
@@ -672,15 +758,7 @@
     bars = jnp.concatenate([weight * slope, weight * bend * hidden[own_rows:]], 0)
     r.cot[...] = dot3(bars, r.w_hidden, nt_dims)
     r.put(r.cot)
-    table_cotangents(
-        r.back_ghost,
-        lambda step, slot: at(r.at_ghost, step),
-        r.plain,
-        r.dotted,
-        r.filt_near,
-        r.cot,
-        chunks,
-    )
+    ghost_cotangents(r.back_ghost, r.at_plain, r.at_dot, r.filt_near, r.cot)
     send_groups(r, r.back_ghost, sizes)
 
 
@@ -732,10 +810,6 @@
         r.table,
         ghost_chunks,
     )
-    r.need(r.send_rows, r.w_two_out, r.inner)
-    r.send_near[...] = r.send_rows[...]
-    r.out_near[...] = r.w_two_out[...]
-    r.inner_near[...] = r.inner[...]
 
 
 def pairs_again(r, geo, osc, phi, chunks):
@@ -759,16 +833,15 @@
     channels = r.back.shape[1] // 2
     r.table[...] = jnp.zeros_like(r.table)
     receive(r, r.table, sizes)
-    add_returned(r.back, r.table, r.send_near[...])
-    r.need(r.w_two_in, r.cot)
+    add_returned(r.back, r.table, r.send_rows[...])
     outer = dot3(
-        jnp.concatenate([r.back[:, :channels], r.back[:, channels:]], 0), r.out_near, nt_dims
-    )
-    _, slope, bend = silu_parts(r.inner_near[:own_rows, :])
+        jnp.concatenate([r.back[:, :channels], r.back[:, channels:]], 0), r.w_two_out, nt_dims
+    )
+    _, slope, bend = silu_parts(r.inner[:own_rows, :])
     pulled = jnp.concatenate(
         [
             outer[:own_rows] * slope,
-            outer[own_rows:] * slope + outer[:own_rows] * bend * r.inner_near[own_rows:, :],
+            outer[own_rows:] * slope + outer[:own_rows] * bend * r.inner[own_rows:, :],
         ],
         0,
     )
@@ -777,7 +850,7 @@
     half = 3 * own_rows
     maps = r.maps
     bar, bar_dot = bars[0:own_rows], bars[own_rows:]
-    r.need(r.maps, r.w_left, r.w_right)
+    r.need(r.w_left, r.w_right)
     for i in range(3):
         a, b = i * own_rows, (i + 1) * own_rows
         left, left_dot = maps[a:b, :], maps[half + a : half + b, :]
@@ -873,7 +946,7 @@
         object.__setattr__(self, name, Slot(name, value))
 
 
-def call(kernel, v, loads, outs, scratch, index=(), raw=(), scalars=(), sent=(), near=None):
+def call(kernel, v, loads, outs, scratch, index=(), raw=(), scalars=(), sent=(), near=None, carry=()):
     near = near or dict()
     raw = raw + tuple(slot for slot in loads if slot.near)
     loads = tuple(slot for slot in loads if not slot.near)
@@ -896,6 +969,13 @@
             buffers.append(pltpu.VMEM(shape, kind))
             copies += 1
     places = [pltpu.HBM] * len(shapes)
+    for slot in carry:
+        array = slot.arrays[0]
+        args.append(pltpu.with_memory_space_constraint(array, pltpu.HBM))
+        kinds.append(pl.BlockSpec(memory_space=pltpu.HBM))
+        shapes.append(jax.ShapeDtypeStruct(array.shape, array.dtype))
+        places.append(pltpu.VMEM)
+        copies += 1
     for entry in near.values():
         for shape, kind in flat(entry):
             shapes.append(jax.ShapeDtypeStruct(shape, kind))
@@ -940,6 +1020,12 @@
             for buffer in group:
                 copy = pltpu.make_async_copy(buffer, targets.pop(0), sems.pop(0))
                 r.stores[key].append(copy)
+        for slot in carry:
+            buffer = targets.pop(0)
+            setattr(r, slot.name, buffer)
+            copy = pltpu.make_async_copy(ins.pop(0), buffer, sems.pop(0))
+            copy.start()
+            r.loads[id(buffer)] = [copy]
         for name, entry in near.items():
             group = tuple(targets.pop(0) for _ in flat(entry))
             setattr(r, name, group if len(group) > 1 else group[0])
@@ -963,11 +1049,16 @@
     for name, (shape, types) in outs.items():
         group = tuple(results.pop(0) for _ in as_tuple(types))
         setattr(v, name, group)
+    carried = Slots()
+    for slot in carry:
+        setattr(carried, slot.name, results.pop(0))
+        getattr(carried, slot.name).near = True
     for name, entry in near.items():
         setattr(v, name, tuple(results.pop(0) for _ in flat(entry)))
         getattr(v, name).near = True
     if sent:
         v.arrived = exchanged(results.pop(0))
+    return carried
 
 
 def exchanged(buffer):
@@ -1035,7 +1126,7 @@
     call(
         part(first_own_kernel, scale, own_chunks),
         v,
-        (v.positions, v.tangent, v.neighbours, v.w_one_in, v.w_one_out, v.embedding, v.filter_one, v.filter_two),
+        (v.positions, v.tangent, v.neighbours, v.w_one_in, v.w_one_out, v.embedding, v.filter_one, v.filter_two, v.send_rows),
         dict(
             box=((n, n), f32),
             cols=((n, n), f32),
@@ -1046,6 +1137,7 @@
             geo_own=geometry,
             osc_own=osc,
             phi_own=((n, 2 * channels), f32),
+            acc=((8 * n, channels), f32),
         ),
         dict(
             gs=factors(2),
@@ -1055,69 +1147,102 @@
             work=((2, 8 * n, wide), pair),
         ),
         near=dict(
-            acc=((8 * n, channels), f32),
-            cols_near=((n, n), f32),
-            mask_near=((ghosts, n), f32),
+            acc_sent=((8 * ghosts, channels), f32),
+            cols_sent=((ghosts, n), f32),
+            emb_sent=((ghosts, channels), f32),
+            wbox_sent=((ghosts, lanes), f32),
             filt_near=((orders, 2 * channels), f32),
             in_near=((channels, channels), f32),
             out_near=((channels, 2 * channels), f32),
         ),
     )
     call(
-        part(first_ghost_kernel, sizes, ghost_chunks),
+        part(first_sent_kernel, sizes, ghost_chunks),
         v,
-        (v.cols_near, v.mask_near, v.filt_near, v.in_near, v.out_near, v.acc, v.w_left, v.w_right, v.embedding, v.w_two_in, v.w_two_out),
+        (
+            v.acc_sent,
+            v.cols_sent,
+            v.emb_sent,
+            v.wbox_sent,
+            v.filt_near,
+            v.in_near,
+            v.out_near,
+            v.w_left,
+            v.w_right,
+            v.w_two_in,
+            v.w_two_out,
+        ),
         dict(
-            node=((2 * n, channels), f32),
-            inner=((2 * n, channels), f32),
-            maps=((12 * n, channels), f32),
-            phi_two=((n, 2 * channels), f32),
             phi_ghost=((ghosts, 2 * channels), f32),
             coords_ghost=((ghosts, lanes), f32),
         ),
         dict(
-            geo=geometry,
-            osc=osc,
+            geo=((geo_slots, ghosts, lanes), f32),
+            osc=((osc_slots, ghosts, lanes), f32),
             gs=factors(2),
             gv=factors(2),
-            wbox=wbox,
-            state=state,
-            work=((2, 8 * n, wide), pair),
+            state=[((2, ghosts, wide), f32), ((2, ghosts, lanes), f32)],
+            work=((2, 8 * ghosts, wide), pair),
+            node=((2 * ghosts, channels), f32),
+            inner=((2 * ghosts, channels), f32),
+            maps=((12 * ghosts, channels), f32),
             table=((ghosts, channels + lanes), f32),
             stage=((ghosts, 2 * channels), f32),
         ),
-        index=(v.send_rows,),
         raw=(v.arrived,),
         sent=(devices, count, 2 * channels),
     )
     call(
         part(second_own_kernel, own_chunks, ghost_chunks),
         v,
-        (v.geo_own, v.osc_own, v.phi_two, v.filt_two, v.box, v.cols, v.mask_own, v.mask_ghost, v.coords_ghost),
+        (
+            v.cols,
+            v.mask_ghost,
+            v.coords_ghost,
+            v.phi_ghost,
+            v.filt_one,
+            v.acc,
+            v.w_left,
+            v.w_right,
+            v.embedding,
+            v.w_two_in,
+            v.w_two_out,
+            v.geo_own,
+            v.osc_own,
+            v.filt_two,
+            v.box,
+            v.mask_own,
+        ),
         dict(
             geo_ghost=geometry,
             osc_ghost=osc,
+            maps=((12 * n, channels), f32),
+            node=((2 * n, channels), f32),
+            inner=((2 * n, channels), f32),
+            phi_two=((n, 2 * channels), f32),
         ),
         dict(
             geo=geometry,
             osc=osc,
             state=state,
             wbox=wbox,
+            work_one=((2, 8 * n, wide), pair),
             work=((2, 2 * n, wide), pair),
-            plain=factors(2),
-            dotted=factors(2),
+            gs=factors(2),
+            gv=factors(2),
         ),
         near=dict(
             acc_two=((2 * n, channels), f32),
-            at_ghost=((own_chunks, 2 * ghosts, wide), pair),
+            at_plain=((orders, ghosts, wide), bf16),
+            at_dot=((orders, ghosts, wide), bf16),
             a_ghost=((ghost_chunks, 2 * n, wide), pair),
             filt_near=((orders, channels), f32),
         ),
     )
     call(
-        part(second_ghost_kernel, sizes, own_chunks, ghost_chunks),
+        part(second_ghost_kernel, sizes, ghost_chunks),
         v,
-        (v.filt_near, v.acc_two, v.a_ghost, v.node, v.w_hidden, v.w_energy, v.at_ghost),
+        (v.filt_near, v.acc_two, v.a_ghost, v.node, v.w_hidden, v.w_energy, v.at_plain, v.at_dot),
         dict(
             cot=((2 * n, channels), f32),
             table=((ghosts, 2 * channels), f32),
@@ -1131,10 +1256,10 @@
         scalars=(v.counts,),
         sent=(devices, count, 2 * channels),
     )
-    call(
+    carried = call(
         part(second_back_kernel, own_chunks, ghost_chunks),
         v,
-        (v.box, v.cols, v.mask_own, v.cot, v.filt_two, v.geo_own, v.osc_own, v.phi_two, v.table, v.geo_ghost, v.osc_ghost, v.send_rows, v.w_two_out, v.inner),
+        (v.box, v.cols, v.mask_own, v.filt_two, v.geo_own, v.osc_own, v.phi_two, v.table, v.geo_ghost, v.osc_ghost),
         dict(
             pair_own=((2, n, lanes), f32),
         ),
@@ -1151,15 +1276,13 @@
         near=dict(
             back=((n, 2 * channels), f32),
             pair_ghost=((2, n, lanes), f32),
-            send_near=((1, ghosts), jnp.int32),
-            out_near=((channels, channels), f32),
-            inner_near=((2 * n, channels), f32),
-        ),
+        ),
+        carry=(v.cot, v.send_rows, v.w_two_out, v.inner, v.w_two_in, v.maps),
     )
     call(
         part(first_back_ghost_kernel, sizes, ghost_chunks),
         v,
-        (v.send_near, v.back, v.out_near, v.inner_near, v.w_two_in, v.cot, v.maps, v.w_left, v.w_right, v.phi_ghost, v.filt_one, v.osc_ghost, v.geo_ghost, v.pair_ghost),
+        (carried.send_rows, v.back, carried.w_two_out, carried.inner, carried.w_two_in, carried.cot, carried.maps, v.w_left, v.w_right, v.phi_ghost, v.filt_one, v.osc_ghost, v.geo_ghost, v.pair_ghost),
         dict(
             bars=((8 * n, channels), pair),
             by_atom=((n, lanes), f32),
@@ -1179,7 +1302,7 @@
     call(
         part(first_back_own_kernel, own_chunks),
         v,
-        (v.phi_own, v.filt_one, v.geo_own, v.osc_own, v.bars, v.pair_own, v.by_atom, v.send_rows),
+        (v.bars, v.phi_own, v.filt_one, v.geo_own, v.osc_own, v.pair_own, v.by_atom, v.send_rows),
         dict(),
         dict(
             atoms=((n, lanes), f32),

time: 91.1 us -> 88.6 us (0.973)
  waiting for transfers between devices: 14.4 us -> 8.02 us
  Pallas kernels: 56.5 us -> 59 us
  starting transfers between devices: 17 us -> 18.3 us
    all_to_all x4, waiting for transfers between devices: 14.4 us -> 8.02 us  [exchanged(): return lax.all_to_all(buffer, ('bx', 'by'), 0, 0)]
    pallas_call x9, Pallas kernels: 56.5 us -> 59 us  [call(): pl.pallas_call(run, out_shape=shapes, in_specs=kinds, out_specs=[pl.Block...]
    all_to_all x4, starting transfers between devices: 17 us -> 18.3 us  [exchanged(): return lax.all_to_all(buffer, ('bx', 'by'), 0, 0)]
  transfers between devices with their start and end apart: 4 -> 4, of which waited for: 3 -> 3; matrix products, arithmetic and copies ran while one was open for 0% -> 0% of each run, Pallas kernels for 38% -> 46%
where the time goes in v2:
time: 88.6 us; the launch traced here: 86.9 us
  Pallas kernels  59 us (67%)
  starting transfers between devices  18.3 us (21%)
  waiting for transfers between devices  8.02 us (9%)
  between operations  1.56 us (2%)
    pallas_call x9, Pallas kernels, call(): pl.pallas_call(run, out_shape=shapes, in_specs=kinds, out_specs=[pl.Block...  59 us
    all_to_all x4, starting transfers between devices, exchanged(): return lax.all_to_all(buffer, ('bx', 'by'), 0, 0)  18.3 us
    all_to_all x4, waiting for transfers between devices, exchanged(): return lax.all_to_all(buffer, ('bx', 'by'), 0, 0)  8.02 us
  transfers between devices with their start and end apart: 4, of which 3 were waited for; matrix products, arithmetic and copies ran while one was open for 0% of the time, Pallas kernels for 46%

profile of v2, /device:TPU:4, one launch (start us, length us, event | category | flops | bytes accessed | tf_op | source)
XLA Modules:
  0.0 86.9 jit_solution(986543917580908952)
XLA Ops:
  0.6 1.9 %pack_kernel.1 = f32[32,1,2176]{2,1,0:T(1,128)} custom-call(f32[3,128]{1,0:T(4,128)} %refs_0_.5, f32[3,128]{1,0:T(4,128)} %refs_1_.6, f32[128,256]{1,0:T(8,128)} %refs_8_.4, s32[1,64]{1,0:T(1,128)} %refs_8_.5), custom_call_target="tpu_custom_call" | custom-call | tf_op jit(solution)/shard_map/pack_kernel/pallas_call | solution.py:1039
  2.5 6.1 %all-to-all-start = ((f32[32,1,2176]{2,1,0:T(1,128)}), f32[32,1,2176]{2,1,0:T(1,128)S(1)}, u32[]{:S(2)}, u32[]{:S(2)}) async-start(f32[32,1,2176]{2,1,0:T(1,128)} %pack_kernel.1), calls=%async_computation | async-start | bytes 557056 | tf_op jit(solution)/shard_map/all_to_all | solution.py:1065
  8.6 9.2 %first_own_kernel.1 = (f32[128,128]{1,0:T(8,128)}, f32[128,128]{1,0:T(8,128)}, f32[128,128]{1,0:T(8,128)}, f32[64,128]{1,0:T(8,128)}, f32[20,512]{1,0:T(8,128)},...) custom-call(f32[3,128]{1,0:T(4,128)} %refs_0_.5, ...), custom_call_target="tpu_custom_call" | custom-call | tf_op jit(solution)/shard_map/first_own_kernel/pallas_call | solution.py:1039
  17.8 0.9 %all-to-all-done.refs_4_ = f32[32,1,2176]{2,1,0:T(1,128)S(1)} async-done(((f32[32,1,2176]{2,1,0:T(1,128)}), f32[32,1,2176]{2,1,0:T(1,128)S(1)}, u32[]{:S(2)}, u32[]{:S(2)}) %all-to-all-start) | async-done | bytes 278560 | tf_op jit(solution)/shard_map/all_to_all | solution.py:1065
  18.7 4.6 %first_sent_kernel.1 = (f32[64,512]{1,0:T(8,128)}, f32[64,128]{1,0:T(8,128)}, f32[32,8,512]{2,1,0:T(8,128)}) custom-call(f32[256,256]{1,0:T(8,128)} %refs_0_.7, f32[256,256]{1,0:T(8,128)} %refs_1_.9, f32[256,256]{1,0:T(8,128)} %refs_14_.1, f32[256,256]{1,0:T(8,128)} %refs_12_.1, f32[32,1,2176]{2,1,0:T(1,128)S(1)} %all-to-all-done.refs_4_, ...), custom_call_target="tpu_custom_call" | custom-call | tf_op jit(solution)/shard_map/first_sent_kernel/pallas_call | solution.py:1039
  23.2 5.0 %all-to-all-start.1 = ((f32[32,8,512]{2,1,0:T(8,128)}), f32[32,8,512]{2,1,0:T(8,128)S(1)}, u32[]{:S(2)}, u32[]{:S(2)}) async-start(f32[32,8,512]{2,1,0:T(8,128)} %get-tuple-element.73), calls=%async_computation.1 | async-start | bytes 1048576 | tf_op jit(solution)/shard_map/all_to_all | solution.py:1065
  28.9 11.3 %second_own_kernel.1 = (f32[8,128,128]{2,1,0:T(8,128)}, f32[5,128,128]{2,1,0:T(8,128)}, f32[1536,256]{1,0:T(8,128)}, f32[256,256]{1,0:T(8,128)}, f32[256,256]{1,...) custom-call(f32[128,128]{1,0:T(8,128)} %get-tuple-element.61.refs_0_, ...), custom_call_target="tpu_custom_call" | custom-call | tf_op jit(solution)/shard_map/second_own_kernel/pallas_call | solution.py:1039
  40.2 3.0 %all-to-all-done.1.refs_3_ = f32[32,8,512]{2,1,0:T(8,128)S(1)} async-done(((f32[32,8,512]{2,1,0:T(8,128)}), f32[32,8,512]{2,1,0:T(8,128)S(1)}, u32[]{:S(2)}, u32[]{:S(2)}) %all-to-all-start.1) | async-done | bytes 524320 | tf_op jit(solution)/shard_map/all_to_all | solution.py:1065
  43.3 4.9 %second_ghost_kernel.1 = (f32[256,256]{1,0:T(8,128)}, f32[64,512]{1,0:T(8,128)}, f32[32,8,512]{2,1,0:T(8,128)}) custom-call(f32[256,256]{1,0:T(8,128)} %get-tuple-element.72.refs_0_, f32[256,256]{1,0:T(8,128)} %refs_1_.8, f32[1,256]{1,0:T(1,128)} %bitcast.1, f32[32,8,512]{2,1,0:T(8,128)S(1)} %all-to-all-done.1.refs_3_, ...), custom_call_target="tpu_custom_call" | custom-call | tf_op jit(solution)/shard_map/second_ghost_kernel/pallas_call | solution.py:1039
  48.2 3.6 %all-to-all-start.2 = ((f32[32,8,512]{2,1,0:T(8,128)}), f32[32,8,512]{2,1,0:T(8,128)S(1)}, u32[]{:S(2)}, u32[]{:S(2)}) async-start(f32[32,8,512]{2,1,0:T(8,128)} %get-tuple-element.80), calls=%async_computation.2 | async-start | bytes 1048576 | tf_op jit(solution)/shard_map/all_to_all | solution.py:1065
  51.8 10.9 %second_back_kernel.1 = (f32[2,128,128]{2,1,0:T(8,128)}, f32[256,256]{1,0:T(8,128)S(1)}, s32[1,64]{1,0:T(1,128)S(1)}, f32[256,256]{1,0:T(8,128)S(1)}, f32[256,25...) custom-call(f32[128,128]{1,0:T(8,128)} %get-tuple-element.68.refs_14, ...), custom_call_target="tpu_custom_call" | custom-call | tf_op jit(solution)/shard_map/second_back_kernel/pallas_call | solution.py:1039
  62.7 4.1 %all-to-all-done.2.refs_6_ = f32[32,8,512]{2,1,0:T(8,128)S(1)} async-done(((f32[32,8,512]{2,1,0:T(8,128)}), f32[32,8,512]{2,1,0:T(8,128)S(1)}, u32[]{:S(2)}, u32[]{:S(2)}) %all-to-all-start.2) | async-done | bytes 524320 | tf_op jit(solution)/shard_map/all_to_all | solution.py:1065
  66.8 6.5 %first_back_ghost_kernel.1 = (bf16[1024,256]{1,0:T(8,128)(2,1)}, bf16[1024,256]{1,0:T(8,128)(2,1)}, f32[128,128]{1,0:T(8,128)}, f32[32,8,128]{2,1,0:T(8,128)}) custom-call(f32[256,256]{1,0:T(8,128)} %refs_0_.7, f32[256,256]{1,0:T(8,128)} %refs_1_.9, f32[64,512]{1,0:T(8,128)} %get-tuple-element.59.refs_3_.refs_2_, ...), custom_call_target="tpu_custom_call" | custom-call | tf_op jit(solution)/shard_map/first_back_ghost_kernel/pallas_call | solution.py:1039
  73.4 3.6 %all-to-all-start.3 = ((f32[32,8,128]{2,1,0:T(8,128)}), f32[32,8,128]{2,1,0:T(8,128)S(1)}, u32[]{:S(2)}, u32[]{:S(2)}) async-start(f32[32,8,128]{2,1,0:T(8,128)} %get-tuple-element.94), calls=%async_computation.3 | async-start | bytes 262144 | tf_op jit(solution)/shard_map/all_to_all | solution.py:1065
  77.0 8.7 %first_back_own_kernel.1 = (f32[8,128]{1,0:T(8,128)S(1)}, s32[1,64]{1,0:T(1,128)S(1)}) custom-call(bf16[1024,256]{1,0:T(8,128)(2,1)} %get-tuple-element.95.refs_0_, bf16[1024,256]{1,0:T(8,128)(2,1)} %get-tuple-element.96.refs_1_, f32[128,512]{1,0:T(8,128)} %get-tuple-element.97.refs_2_, f32[20,512]{1,0:T(8,128)} %get-tuple-element.60.refs_4_.refs_3_, ...), custom_call_target="tpu_custom_call" | custom-call | tf_op jit(solution)/shard_map/first_back_own_kernel/pallas_call | solution.py:1039
  85.7 0.0 all-to-all-done.3.refs_0_
  85.7 1.0 %finish_kernel.1 = (f32[3,128]{1,0:T(4,128)}, f32[3,128]{1,0:T(4,128)}) custom-call(f32[32,8,128]{2,1,0:T(8,128)S(1)} %all-to-all-done.3.refs_0_, s32[1,64]{1,0:T(1,128)S(1)} %get-tuple-element.100.refs_1_, f32[8,128]{1,0:T(8,128)S(1)} %get-tuple-element.101.refs_2_), custom_call_target="tpu_custom_call" | custom-call | tf_op jit(solution)/shard_map/finish_kernel/pallas_call | solution.py:1039
Async XLA Ops:
  2.5 16.1 %all-to-all-start = ((f32[32,1,2176]{2,1,0:T(1,128)}), f32[32,1,2176]{2,1,0:T(1,128)S(1)}, u32[]{:S(2)}, u32[]{:S(2)}) async-start(f32[32,1,2176]{2,1,0:T(1,128)} %pack_kernel.1), calls=%async_computation | async-start | bytes 557056 | tf_op jit(solution)/shard_map/all_to_all | solution.py:1065
  23.2 20.0 %all-to-all-start.1 = ((f32[32,8,512]{2,1,0:T(8,128)}), f32[32,8,512]{2,1,0:T(8,128)S(1)}, u32[]{:S(2)}, u32[]{:S(2)}) async-start(f32[32,8,512]{2,1,0:T(8,128)} %get-tuple-element.73), calls=%async_computation.1 | async-start | bytes 1048576 | tf_op jit(solution)/shard_map/all_to_all | solution.py:1065
  48.2 18.7 %all-to-all-start.2 = ((f32[32,8,512]{2,1,0:T(8,128)}), f32[32,8,512]{2,1,0:T(8,128)S(1)}, u32[]{:S(2)}, u32[]{:S(2)}) async-start(f32[32,8,512]{2,1,0:T(8,128)} %get-tuple-element.80), calls=%async_computation.2 | async-start | bytes 1048576 | tf_op jit(solution)/shard_map/all_to_all | solution.py:1065
  73.4 12.4 %all-to-all-start.3 = ((f32[32,8,128]{2,1,0:T(8,128)}), f32[32,8,128]{2,1,0:T(8,128)S(1)}, u32[]{:S(2)}, u32[]{:S(2)}) async-start(f32[32,8,128]{2,1,0:T(8,128)} %get-tuple-element.94), calls=%async_computation.3 | async-start | bytes 262144 | tf_op jit(solution)/shard_map/all_to_all | solution.py:1065

commit v3 on v2

--- a/solution.py
+++ b/solution.py
@@ -145,8 +145,8 @@
     waves[1, rows, :] = c * rc - s * rs
 
 
-def steps(count, members, body):
-    group = own_group if members == lanes else ghost_group
+def steps(count, members, body, group=None):
+    group = group or (own_group if members == lanes else ghost_group)
     if group >= count:
         for step in range(count):
             body(step, step % 2)
@@ -256,7 +256,7 @@
         acc[:top, :] += three(ah[:top, :], al[:top, :], scalars[0][slot], scalars[1][slot])
         acc[top:, :] += three(ah[top:, :], al[top:, :], vectors[0][slot], vectors[1][slot])
 
-    steps(chunks, members, chunk)
+    steps(chunks, members, chunk, 10)
 
 
 def second_messages(acc, basis_at, plain, dotted, filt, value, chunks):
@@ -315,8 +315,11 @@
     steps(chunks, own_rows, chunk)
 
 
-def folded(value, members):
-    total = value[:, :lanes] + value[:, lanes:]
+def halved(value):
+    return value[:, :lanes] + value[:, lanes:]
+
+
+def folded(total, members):
     if members < lanes:
         total = total + pltpu.roll(total, members, 1)
     return total
@@ -340,8 +343,8 @@
             rows = pl.ds(start, row_block)
             _, b1, b2d = basis(rows)
             g = both[start : start + row_block]
-            pair[0, rows, :] += b1 * g
-            pair[1, rows, :] += b2d * g + b1 * dot[start : start + row_block]
+            pair[0, rows, :] += halved(b1 * g)
+            pair[1, rows, :] += halved(b2d * g + b1 * dot[start : start + row_block])
 
     members = value.shape[0]
     steps(chunks, members, chunk)
@@ -379,10 +382,10 @@
                 unit = doubled(geo[U + i, rows, :])
                 along = along + unit * g
                 along_dot = along_dot + unit * gd + doubled(geo[UD + i, rows, :]) * g
-                pair[2 + i, rows, :] += b * g
-                pair[5 + i, rows, :] += b * gd + b1d * g
-            pair[0, rows, :] += b1 * along
-            pair[1, rows, :] += b2d * along + b1 * along_dot
+                pair[2 + i, rows, :] += halved(b * g)
+                pair[5 + i, rows, :] += halved(b * gd + b1d * g)
+            pair[0, rows, :] += halved(b1 * along)
+            pair[1, rows, :] += halved(b2d * along + b1 * along_dot)
 
     steps(chunks, members, chunk)
 
@@ -1107,7 +1110,7 @@
     osc = ((osc_slots, n, lanes), f32)
     state = [((2, n, wide), f32), ((2, n, lanes), f32)]
     wbox = ((n, lanes), f32)
-    pairs = ((8, n, wide), f32)
+    pairs = ((8, n, lanes), f32)
     cots = ((2, 8 * n, wide), f32)
 
     call(
@@ -1271,7 +1274,7 @@
             work=((2, 2 * n, wide), pair),
             plain=factors(2),
             dotted=factors(2),
-            pair=((2, n, wide), f32),
+            pair=((2, n, lanes), f32),
         ),
         near=dict(
             back=((n, 2 * channels), f32),

time: 88.6 us -> 87.4 us (0.986)
  Pallas kernels: 59 us -> 57.8 us
    pallas_call x9, Pallas kernels: 59 us -> 57.8 us  [call(): pl.pallas_call(run, out_shape=shapes, in_specs=kinds, out_specs=[pl.Block...]
where the time goes in v3:
time: 87.4 us; the launch traced here: 85.7 us
  Pallas kernels  57.8 us (66%)
  starting transfers between devices  17.5 us (20%)
  waiting for transfers between devices  8.86 us (10%)
  between operations  1.56 us (2%)
    pallas_call x9, Pallas kernels, call(): pl.pallas_call(run, out_shape=shapes, in_specs=kinds, out_specs=[pl.Block...  57.8 us
    all_to_all x4, starting transfers between devices, exchanged(): return lax.all_to_all(buffer, ('bx', 'by'), 0, 0)  17.5 us
    all_to_all x4, waiting for transfers between devices, exchanged(): return lax.all_to_all(buffer, ('bx', 'by'), 0, 0)  8.86 us
  transfers between devices with their start and end apart: 4, of which 3 were waited for; matrix products, arithmetic and copies ran while one was open for 0% of the time, Pallas kernels for 46%

profile of v3, /device:TPU:4, one launch (start us, length us, event | category | flops | bytes accessed | tf_op | source)
XLA Modules:
  0.0 85.7 jit_solution(15225878709683978912)
XLA Ops:
  0.6 1.9 %pack_kernel.1 = f32[32,1,2176]{2,1,0:T(1,128)} custom-call(f32[3,128]{1,0:T(4,128)} %refs_0_.5, f32[3,128]{1,0:T(4,128)} %refs_1_.6, f32[128,256]{1,0:T(8,128)} %refs_8_.4, s32[1,64]{1,0:T(1,128)} %refs_8_.5), custom_call_target="tpu_custom_call" | custom-call | tf_op jit(solution)/shard_map/pack_kernel/pallas_call | solution.py:1042
  2.5 6.1 %all-to-all-start = ((f32[32,1,2176]{2,1,0:T(1,128)}), f32[32,1,2176]{2,1,0:T(1,128)S(1)}, u32[]{:S(2)}, u32[]{:S(2)}) async-start(f32[32,1,2176]{2,1,0:T(1,128)} %pack_kernel.1), calls=%async_computation | async-start | bytes 557056 | tf_op jit(solution)/shard_map/all_to_all | solution.py:1068
  8.6 8.3 %first_own_kernel.1 = (f32[128,128]{1,0:T(8,128)}, f32[128,128]{1,0:T(8,128)}, f32[128,128]{1,0:T(8,128)}, f32[64,128]{1,0:T(8,128)}, f32[20,512]{1,0:T(8,128)},...) custom-call(f32[3,128]{1,0:T(4,128)} %refs_0_.5, ...), custom_call_target="tpu_custom_call" | custom-call | tf_op jit(solution)/shard_map/first_own_kernel/pallas_call | solution.py:1042
  17.0 1.7 %all-to-all-done.refs_4_ = f32[32,1,2176]{2,1,0:T(1,128)S(1)} async-done(((f32[32,1,2176]{2,1,0:T(1,128)}), f32[32,1,2176]{2,1,0:T(1,128)S(1)}, u32[]{:S(2)}, u32[]{:S(2)}) %all-to-all-start) | async-done | bytes 278560 | tf_op jit(solution)/shard_map/all_to_all | solution.py:1068
  18.7 4.6 %first_sent_kernel.1 = (f32[64,512]{1,0:T(8,128)}, f32[64,128]{1,0:T(8,128)}, f32[32,8,512]{2,1,0:T(8,128)}) custom-call(f32[256,256]{1,0:T(8,128)} %refs_0_.7, f32[256,256]{1,0:T(8,128)} %refs_1_.9, f32[256,256]{1,0:T(8,128)} %refs_14_.1, f32[256,256]{1,0:T(8,128)} %refs_12_.1, f32[32,1,2176]{2,1,0:T(1,128)S(1)} %all-to-all-done.refs_4_, ...), custom_call_target="tpu_custom_call" | custom-call | tf_op jit(solution)/shard_map/first_sent_kernel/pallas_call | solution.py:1042
  23.2 4.2 %all-to-all-start.1 = ((f32[32,8,512]{2,1,0:T(8,128)}), f32[32,8,512]{2,1,0:T(8,128)S(1)}, u32[]{:S(2)}, u32[]{:S(2)}) async-start(f32[32,8,512]{2,1,0:T(8,128)} %get-tuple-element.73), calls=%async_computation.1 | async-start | bytes 1048576 | tf_op jit(solution)/shard_map/all_to_all | solution.py:1068
  28.1 11.3 %second_own_kernel.1 = (f32[8,128,128]{2,1,0:T(8,128)}, f32[5,128,128]{2,1,0:T(8,128)}, f32[1536,256]{1,0:T(8,128)}, f32[256,256]{1,0:T(8,128)}, f32[256,256]{1,...) custom-call(f32[128,128]{1,0:T(8,128)} %get-tuple-element.61.refs_0_, ...), custom_call_target="tpu_custom_call" | custom-call | tf_op jit(solution)/shard_map/second_own_kernel/pallas_call | solution.py:1042
  39.4 3.0 %all-to-all-done.1.refs_3_ = f32[32,8,512]{2,1,0:T(8,128)S(1)} async-done(((f32[32,8,512]{2,1,0:T(8,128)}), f32[32,8,512]{2,1,0:T(8,128)S(1)}, u32[]{:S(2)}, u32[]{:S(2)}) %all-to-all-start.1) | async-done | bytes 524320 | tf_op jit(solution)/shard_map/all_to_all | solution.py:1068
  42.4 4.9 %second_ghost_kernel.1 = (f32[256,256]{1,0:T(8,128)}, f32[64,512]{1,0:T(8,128)}, f32[32,8,512]{2,1,0:T(8,128)}) custom-call(f32[256,256]{1,0:T(8,128)} %get-tuple-element.72.refs_0_, f32[256,256]{1,0:T(8,128)} %refs_1_.8, f32[1,256]{1,0:T(1,128)} %bitcast.1, f32[32,8,512]{2,1,0:T(8,128)S(1)} %all-to-all-done.1.refs_3_, ...), custom_call_target="tpu_custom_call" | custom-call | tf_op jit(solution)/shard_map/second_ghost_kernel/pallas_call | solution.py:1042
  47.3 3.6 %all-to-all-start.2 = ((f32[32,8,512]{2,1,0:T(8,128)}), f32[32,8,512]{2,1,0:T(8,128)S(1)}, u32[]{:S(2)}, u32[]{:S(2)}) async-start(f32[32,8,512]{2,1,0:T(8,128)} %get-tuple-element.80), calls=%async_computation.2 | async-start | bytes 1048576 | tf_op jit(solution)/shard_map/all_to_all | solution.py:1068
  51.0 10.9 %second_back_kernel.1 = (f32[2,128,128]{2,1,0:T(8,128)}, f32[256,256]{1,0:T(8,128)S(1)}, s32[1,64]{1,0:T(1,128)S(1)}, f32[256,256]{1,0:T(8,128)S(1)}, f32[256,25...) custom-call(f32[128,128]{1,0:T(8,128)} %get-tuple-element.68.refs_14, ...), custom_call_target="tpu_custom_call" | custom-call | tf_op jit(solution)/shard_map/second_back_kernel/pallas_call | solution.py:1042
  61.8 4.1 %all-to-all-done.2.refs_6_ = f32[32,8,512]{2,1,0:T(8,128)S(1)} async-done(((f32[32,8,512]{2,1,0:T(8,128)}), f32[32,8,512]{2,1,0:T(8,128)S(1)}, u32[]{:S(2)}, u32[]{:S(2)}) %all-to-all-start.2) | async-done | bytes 524320 | tf_op jit(solution)/shard_map/all_to_all | solution.py:1068
  66.0 6.4 %first_back_ghost_kernel.1 = (bf16[1024,256]{1,0:T(8,128)(2,1)}, bf16[1024,256]{1,0:T(8,128)(2,1)}, f32[128,128]{1,0:T(8,128)}, f32[32,8,128]{2,1,0:T(8,128)}) custom-call(f32[256,256]{1,0:T(8,128)} %refs_0_.7, f32[256,256]{1,0:T(8,128)} %refs_1_.9, f32[64,512]{1,0:T(8,128)} %get-tuple-element.59.refs_3_.refs_2_, ...), custom_call_target="tpu_custom_call" | custom-call | tf_op jit(solution)/shard_map/first_back_ghost_kernel/pallas_call | solution.py:1042
  72.4 3.6 %all-to-all-start.3 = ((f32[32,8,128]{2,1,0:T(8,128)}), f32[32,8,128]{2,1,0:T(8,128)S(1)}, u32[]{:S(2)}, u32[]{:S(2)}) async-start(f32[32,8,128]{2,1,0:T(8,128)} %get-tuple-element.94), calls=%async_computation.3 | async-start | bytes 262144 | tf_op jit(solution)/shard_map/all_to_all | solution.py:1068
  76.1 8.5 %first_back_own_kernel.1 = (f32[8,128]{1,0:T(8,128)S(1)}, s32[1,64]{1,0:T(1,128)S(1)}) custom-call(bf16[1024,256]{1,0:T(8,128)(2,1)} %get-tuple-element.95.refs_0_, bf16[1024,256]{1,0:T(8,128)(2,1)} %get-tuple-element.96.refs_1_, f32[128,512]{1,0:T(8,128)} %get-tuple-element.97.refs_2_, f32[20,512]{1,0:T(8,128)} %get-tuple-element.60.refs_4_.refs_3_, ...), custom_call_target="tpu_custom_call" | custom-call | tf_op jit(solution)/shard_map/first_back_own_kernel/pallas_call | solution.py:1042
  84.5 0.0 all-to-all-done.3.refs_0_
  84.5 1.0 %finish_kernel.1 = (f32[3,128]{1,0:T(4,128)}, f32[3,128]{1,0:T(4,128)}) custom-call(f32[32,8,128]{2,1,0:T(8,128)S(1)} %all-to-all-done.3.refs_0_, s32[1,64]{1,0:T(1,128)S(1)} %get-tuple-element.100.refs_1_, f32[8,128]{1,0:T(8,128)S(1)} %get-tuple-element.101.refs_2_), custom_call_target="tpu_custom_call" | custom-call | tf_op jit(solution)/shard_map/finish_kernel/pallas_call | solution.py:1042
Async XLA Ops:
  2.5 16.1 %all-to-all-start = ((f32[32,1,2176]{2,1,0:T(1,128)}), f32[32,1,2176]{2,1,0:T(1,128)S(1)}, u32[]{:S(2)}, u32[]{:S(2)}) async-start(f32[32,1,2176]{2,1,0:T(1,128)} %pack_kernel.1), calls=%async_computation | async-start | bytes 557056 | tf_op jit(solution)/shard_map/all_to_all | solution.py:1068
  23.2 19.2 %all-to-all-start.1 = ((f32[32,8,512]{2,1,0:T(8,128)}), f32[32,8,512]{2,1,0:T(8,128)S(1)}, u32[]{:S(2)}, u32[]{:S(2)}) async-start(f32[32,8,512]{2,1,0:T(8,128)} %get-tuple-element.73), calls=%async_computation.1 | async-start | bytes 1048576 | tf_op jit(solution)/shard_map/all_to_all | solution.py:1068
  47.3 18.7 %all-to-all-start.2 = ((f32[32,8,512]{2,1,0:T(8,128)}), f32[32,8,512]{2,1,0:T(8,128)S(1)}, u32[]{:S(2)}, u32[]{:S(2)}) async-start(f32[32,8,512]{2,1,0:T(8,128)} %get-tuple-element.80), calls=%async_computation.2 | async-start | bytes 1048576 | tf_op jit(solution)/shard_map/all_to_all | solution.py:1068
  72.4 12.1 %all-to-all-start.3 = ((f32[32,8,128]{2,1,0:T(8,128)}), f32[32,8,128]{2,1,0:T(8,128)S(1)}, u32[]{:S(2)}, u32[]{:S(2)}) async-start(f32[32,8,128]{2,1,0:T(8,128)} %get-tuple-element.94), calls=%async_computation.3 | async-start | bytes 262144 | tf_op jit(solution)/shard_map/all_to_all | solution.py:1068

commit v4 on v3

--- a/solution.py
+++ b/solution.py
@@ -16,7 +16,7 @@
 offsets = ((-1, -1), (-1, 0), (-1, 1), (0, -1), (0, 1), (1, -1), (1, 0), (1, 1))
 lanes = 128
 wide = 256
-row_block = 32
+row_block = 64
 nn_dims = (((1,), (0,)), ((), ()))
 nt_dims = (((1,), (1,)), ((), ()))
 
@@ -210,6 +210,10 @@
         pair[1][slot, i * members : (i + 1) * members, :] = l
 
 
+def store_pair(pair, value):
+    put_split(pair, 0, value)
+
+
 def put_split(pair, start, value):
     h, l = split(value)
     pair[0][start : start + value.shape[0], :] = h
@@ -256,7 +260,7 @@
         acc[:top, :] += three(ah[:top, :], al[:top, :], scalars[0][slot], scalars[1][slot])
         acc[top:, :] += three(ah[top:, :], al[top:, :], vectors[0][slot], vectors[1][slot])
 
-    steps(chunks, members, chunk, 10)
+    steps(chunks, members, chunk, chunks)
 
 
 def second_messages(acc, basis_at, plain, dotted, filt, value, chunks):
@@ -398,22 +402,19 @@
     return device, inside
 
 
-def send_chunks(r, chunk_at, sizes):
-    for number, target in enumerate(offsets):
-        device, inside = neighbour_id(target, sizes)
-        copy = pltpu.make_async_copy(chunk_at(number), r.out.at[device], r.moves.at[number])
-
-        @pl.when(inside)
-        def _():
-            copy.start()
-
-    for number, target in enumerate(offsets):
-        device, inside = neighbour_id(target, sizes)
-        copy = pltpu.make_async_copy(chunk_at(number), r.out.at[device], r.moves.at[number])
-
-        @pl.when(inside)
-        def _():
-            copy.wait()
+def send_chunks(r, chunk_at, sizes, beside=lambda: None):
+    def each(act):
+        for number, target in enumerate(offsets):
+            device, inside = neighbour_id(target, sizes)
+            copy = pltpu.make_async_copy(chunk_at(number), r.out.at[device], r.moves.at[number])
+
+            @pl.when(inside)
+            def _():
+                act(copy)
+
+    each(lambda copy: copy.start())
+    beside()
+    each(lambda copy: copy.wait())
 
 
 def send_groups(r, table, sizes):
@@ -445,9 +446,8 @@
     total[...] += mxu(place, high) + mxu(place, low) + mxu(place, rest)
 
 
-def offset_gradients(geo, pair, second, members, by_slot, by_atom):
+def offset_gradients(geo, pair, second, members):
     near = [folded(pair[i], members) for i in range(8)]
-    height = geo.shape[1]
     units = [geo[U + i, :, :lanes] for i in range(3)]
     moves = [geo[UD + i, :, :lanes] for i in range(3)]
     inverse = geo[RI, :, :lanes]
@@ -458,8 +458,7 @@
     inner = units[0] * turn[0] + units[1] * turn[1] + units[2] * turn[2]
     inner_dot = sum(units[i] * turn_dot[i] + moves[i] * turn[i] for i in range(3))
     rate = speed * inverse
-    lane = lax.broadcasted_iota(jnp.int32, (1, lanes), 1)
-    sums = jnp.zeros((height, lanes), f32)
+    grads, dots = [], []
     for i in range(3):
         part = (turn[i] - units[i] * inner) * inverse
         grad = along * units[i] + part
@@ -469,11 +468,24 @@
             + (turn_dot[i] - moves[i] * inner - units[i] * inner_dot) * inverse
             - rate * part
         )
-        for row, value in ((i, grad), (3 + i, grad_dot)):
-            by_slot[row : row + 1, :] = jnp.sum(value, 0, keepdims=True)
-            if members < lanes:
-                value = jnp.where(lane < members, value, 0.0)
-            sums = jnp.where(lane == row, -jnp.sum(value, 1, keepdims=True), sums)
+        grads.append(grad)
+        dots.append(grad_dot)
+    return grads + dots
+
+
+def slot_sums(by_slot, values):
+    by_slot[...] = jnp.zeros_like(by_slot)
+    for row, value in enumerate(values):
+        by_slot[row : row + 1, :] = jnp.sum(value, 0, keepdims=True)
+
+
+def atom_sums(by_atom, values, members):
+    lane = lax.broadcasted_iota(jnp.int32, (1, lanes), 1)
+    sums = jnp.zeros(by_atom.shape, f32)
+    for row, value in enumerate(values):
+        if members < lanes:
+            value = jnp.where(lane < members, value, 0.0)
+        sums = jnp.where(lane == row, -jnp.sum(value, 1, keepdims=True), sums)
     by_atom[...] = sums
 
 
@@ -500,6 +512,11 @@
     send_chunks(r, lambda number: r.stage.at[number], sizes)
 
 
+def projected(features, inner, outer):
+    middle = silu_parts(three(*split(features), inner[0][...], inner[1][...]))[0]
+    return three(*split(middle), outer[0][...], outer[1][...])
+
+
 def first_own_kernel(scale, chunks, r):
     own_rows = r.positions.shape[1]
     ghosts = r.mask_ghost.shape[0]
@@ -519,9 +536,9 @@
     r.filt_two[...] = r.filter_two[...] * scale
     r.put(r.filt_one, r.filt_two)
     r.filt_near[...] = r.filt_one[...]
-    r.in_near[...] = r.w_one_in[...]
-    r.out_near[...] = r.w_one_out[...]
-    r.phi_own[...] = dot3(silu_parts(dot3(r.embedding[...], r.w_one_in))[0], r.w_one_out)
+    store_pair(r.in_near, r.w_one_in[...])
+    store_pair(r.out_near, r.w_one_out[...])
+    r.phi_own[...] = projected(r.embedding[...], r.in_near, r.out_near)
     r.put(r.phi_own)
     r.acc[...] = jnp.zeros_like(r.acc)
     first_messages(
@@ -595,9 +612,7 @@
 
     r.coords_ghost[...] = r.table[:, channels:]
     r.put(r.coords_ghost)
-    r.phi_ghost[...] = dot3(
-        silu_parts(dot3(r.table[:, :channels], r.in_near))[0], r.out_near
-    )
+    r.phi_ghost[...] = projected(r.table[:, :channels], r.in_near, r.out_near)
     r.put(r.phi_ghost)
     geometry_by_atom(
         r.geo, r.osc, r.cols_sent[...], ghost_lanes(r.coords_ghost), r.wbox_sent
@@ -867,20 +882,25 @@
     r.put(r.bars)
     r.need(r.geo_ghost, r.osc_ghost, r.phi_ghost, r.filt_one)
     pairs_again(r, r.geo_ghost, r.osc_ghost, r.phi_ghost, chunks)
-    r.by_slot[...] = jnp.zeros_like(r.by_slot)
     members = r.table.shape[0]
-    offset_gradients(r.geo_ghost, r.pair, r.pair_ghost, members, r.by_slot, r.by_atom)
-    r.put(r.by_atom)
-    send_chunks(r, lambda number: r.by_slot, sizes)
+    values = offset_gradients(r.geo_ghost, r.pair, r.pair_ghost, members)
+    slot_sums(r.by_slot, values)
+
+    def beside():
+        atom_sums(r.by_atom, values, members)
+        r.put(r.by_atom)
+
+    send_chunks(r, lambda number: r.by_slot, sizes, beside)
 
 
 def first_back_own_kernel(chunks, r):
     own_rows = r.by_atom.shape[0]
     r.need(r.phi_own, r.filt_one, r.geo_own, r.osc_own, r.bars)
     pairs_again(r, r.geo_own, r.osc_own, r.phi_own, chunks)
-    r.result[...] = jnp.zeros_like(r.result)
     r.need(r.pair_own, r.by_atom)
-    offset_gradients(r.geo_own, r.pair, r.pair_own, own_rows, r.result, r.atoms)
+    values = offset_gradients(r.geo_own, r.pair, r.pair_own, own_rows)
+    slot_sums(r.result, values)
+    atom_sums(r.atoms, values, own_rows)
     r.result[...] += (r.atoms[...] + r.by_atom[...]).T[0:8, :]
     r.need(r.send_rows)
     r.send_near[...] = r.send_rows[...]
@@ -1155,8 +1175,8 @@
             emb_sent=((ghosts, channels), f32),
             wbox_sent=((ghosts, lanes), f32),
             filt_near=((orders, 2 * channels), f32),
-            in_near=((channels, channels), f32),
-            out_near=((channels, 2 * channels), f32),
+            in_near=((channels, channels), pair),
+            out_near=((channels, 2 * channels), pair),
         ),
     )
     call(

time: 87.4 us -> 87.4 us (level)
  no operation moved by 1% of the time
where the time goes in v4:
time: 87.4 us; the launch traced here: 85.7 us
  Pallas kernels  57.9 us (66%)
  starting transfers between devices  17.5 us (20%)
  waiting for transfers between devices  8.74 us (10%)
  between operations  1.56 us (2%)
    pallas_call x9, Pallas kernels, call(): pl.pallas_call(run, out_shape=shapes, in_specs=kinds, out_specs=[pl.Block...  57.9 us
    all_to_all x4, starting transfers between devices, exchanged(): return lax.all_to_all(buffer, ('bx', 'by'), 0, 0)  17.5 us
    all_to_all x4, waiting for transfers between devices, exchanged(): return lax.all_to_all(buffer, ('bx', 'by'), 0, 0)  8.74 us
  transfers between devices with their start and end apart: 4, of which 3 were waited for; matrix products, arithmetic and copies ran while one was open for 0% of the time, Pallas kernels for 46%

profile of v4, /device:TPU:4, one launch (start us, length us, event | category | flops | bytes accessed | tf_op | source)
XLA Modules:
  0.0 85.7 jit_solution(15232300630493257970)
XLA Ops:
  0.6 1.9 %pack_kernel.1 = f32[32,1,2176]{2,1,0:T(1,128)} custom-call(f32[3,128]{1,0:T(4,128)} %refs_0_.5, f32[3,128]{1,0:T(4,128)} %refs_1_.6, f32[128,256]{1,0:T(8,128)} %refs_8_.4, s32[1,64]{1,0:T(1,128)} %refs_8_.5), custom_call_target="tpu_custom_call" | custom-call | tf_op jit(solution)/shard_map/pack_kernel/pallas_call | solution.py:1062
  2.5 6.1 %all-to-all-start = ((f32[32,1,2176]{2,1,0:T(1,128)}), f32[32,1,2176]{2,1,0:T(1,128)S(1)}, u32[]{:S(2)}, u32[]{:S(2)}) async-start(f32[32,1,2176]{2,1,0:T(1,128)} %pack_kernel.1), calls=%async_computation | async-start | bytes 557056 | tf_op jit(solution)/shard_map/all_to_all | solution.py:1088
  8.6 8.3 %first_own_kernel.1 = (f32[128,128]{1,0:T(8,128)}, f32[128,128]{1,0:T(8,128)}, f32[128,128]{1,0:T(8,128)}, f32[64,128]{1,0:T(8,128)}, f32[20,512]{1,0:T(8,128)},...) custom-call(f32[3,128]{1,0:T(4,128)} %refs_0_.5, ...), custom_call_target="tpu_custom_call" | custom-call | tf_op jit(solution)/shard_map/first_own_kernel/pallas_call | solution.py:1062
  16.9 1.7 %all-to-all-done.refs_4_ = f32[32,1,2176]{2,1,0:T(1,128)S(1)} async-done(((f32[32,1,2176]{2,1,0:T(1,128)}), f32[32,1,2176]{2,1,0:T(1,128)S(1)}, u32[]{:S(2)}, u32[]{:S(2)}) %all-to-all-start) | async-done | bytes 278560 | tf_op jit(solution)/shard_map/all_to_all | solution.py:1088
  18.7 4.6 %first_sent_kernel.1 = (f32[64,512]{1,0:T(8,128)}, f32[64,128]{1,0:T(8,128)}, f32[32,8,512]{2,1,0:T(8,128)}) custom-call(f32[256,256]{1,0:T(8,128)} %refs_0_.7, f32[256,256]{1,0:T(8,128)} %refs_1_.9, f32[256,256]{1,0:T(8,128)} %refs_14_.1, f32[256,256]{1,0:T(8,128)} %refs_12_.1, f32[32,1,2176]{2,1,0:T(1,128)S(1)} %all-to-all-done.refs_4_, ...), custom_call_target="tpu_custom_call" | custom-call | tf_op jit(solution)/shard_map/first_sent_kernel/pallas_call | solution.py:1062
  23.2 4.1 %all-to-all-start.1 = ((f32[32,8,512]{2,1,0:T(8,128)}), f32[32,8,512]{2,1,0:T(8,128)S(1)}, u32[]{:S(2)}, u32[]{:S(2)}) async-start(f32[32,8,512]{2,1,0:T(8,128)} %get-tuple-element.77), calls=%async_computation.1 | async-start | bytes 1048576 | tf_op jit(solution)/shard_map/all_to_all | solution.py:1088
  28.0 11.5 %second_own_kernel.1 = (f32[8,128,128]{2,1,0:T(8,128)}, f32[5,128,128]{2,1,0:T(8,128)}, f32[1536,256]{1,0:T(8,128)}, f32[256,256]{1,0:T(8,128)}, f32[256,256]{1,...) custom-call(f32[128,128]{1,0:T(8,128)} %get-tuple-element.65.refs_0_, ...), custom_call_target="tpu_custom_call" | custom-call | tf_op jit(solution)/shard_map/second_own_kernel/pallas_call | solution.py:1062
  39.5 2.9 %all-to-all-done.1.refs_3_ = f32[32,8,512]{2,1,0:T(8,128)S(1)} async-done(((f32[32,8,512]{2,1,0:T(8,128)}), f32[32,8,512]{2,1,0:T(8,128)S(1)}, u32[]{:S(2)}, u32[]{:S(2)}) %all-to-all-start.1) | async-done | bytes 524320 | tf_op jit(solution)/shard_map/all_to_all | solution.py:1088
  42.4 4.9 %second_ghost_kernel.1 = (f32[256,256]{1,0:T(8,128)}, f32[64,512]{1,0:T(8,128)}, f32[32,8,512]{2,1,0:T(8,128)}) custom-call(f32[256,256]{1,0:T(8,128)} %get-tuple-element.76.refs_0_, f32[256,256]{1,0:T(8,128)} %refs_1_.8, f32[1,256]{1,0:T(1,128)} %bitcast.1, f32[32,8,512]{2,1,0:T(8,128)S(1)} %all-to-all-done.1.refs_3_, ...), custom_call_target="tpu_custom_call" | custom-call | tf_op jit(solution)/shard_map/second_ghost_kernel/pallas_call | solution.py:1062
  47.3 3.6 %all-to-all-start.2 = ((f32[32,8,512]{2,1,0:T(8,128)}), f32[32,8,512]{2,1,0:T(8,128)S(1)}, u32[]{:S(2)}, u32[]{:S(2)}) async-start(f32[32,8,512]{2,1,0:T(8,128)} %get-tuple-element.84), calls=%async_computation.2 | async-start | bytes 1048576 | tf_op jit(solution)/shard_map/all_to_all | solution.py:1088
  50.9 10.9 %second_back_kernel.1 = (f32[2,128,128]{2,1,0:T(8,128)}, f32[256,256]{1,0:T(8,128)S(1)}, s32[1,64]{1,0:T(1,128)S(1)}, f32[256,256]{1,0:T(8,128)S(1)}, f32[256,25...) custom-call(f32[128,128]{1,0:T(8,128)} %get-tuple-element.72.refs_14, ...), custom_call_target="tpu_custom_call" | custom-call | tf_op jit(solution)/shard_map/second_back_kernel/pallas_call | solution.py:1062
  61.8 4.1 %all-to-all-done.2.refs_6_ = f32[32,8,512]{2,1,0:T(8,128)S(1)} async-done(((f32[32,8,512]{2,1,0:T(8,128)}), f32[32,8,512]{2,1,0:T(8,128)S(1)}, u32[]{:S(2)}, u32[]{:S(2)}) %all-to-all-start.2) | async-done | bytes 524320 | tf_op jit(solution)/shard_map/all_to_all | solution.py:1088
  66.0 6.4 %first_back_ghost_kernel.1 = (bf16[1024,256]{1,0:T(8,128)(2,1)}, bf16[1024,256]{1,0:T(8,128)(2,1)}, f32[128,128]{1,0:T(8,128)}, f32[32,8,128]{2,1,0:T(8,128)}) custom-call(f32[256,256]{1,0:T(8,128)} %refs_0_.7, f32[256,256]{1,0:T(8,128)} %refs_1_.9, f32[64,512]{1,0:T(8,128)} %get-tuple-element.63.refs_3_.refs_2_, ...), custom_call_target="tpu_custom_call" | custom-call | tf_op jit(solution)/shard_map/first_back_ghost_kernel/pallas_call | solution.py:1062
  72.4 3.6 %all-to-all-start.3 = ((f32[32,8,128]{2,1,0:T(8,128)}), f32[32,8,128]{2,1,0:T(8,128)S(1)}, u32[]{:S(2)}, u32[]{:S(2)}) async-start(f32[32,8,128]{2,1,0:T(8,128)} %get-tuple-element.98), calls=%async_computation.3 | async-start | bytes 262144 | tf_op jit(solution)/shard_map/all_to_all | solution.py:1088
  76.0 8.5 %first_back_own_kernel.1 = (f32[8,128]{1,0:T(8,128)S(1)}, s32[1,64]{1,0:T(1,128)S(1)}) custom-call(bf16[1024,256]{1,0:T(8,128)(2,1)} %get-tuple-element.99.refs_0_, bf16[1024,256]{1,0:T(8,128)(2,1)} %get-tuple-element.100.refs_1_, f32[128,512]{1,0:T(8,128)} %get-tuple-element.101.refs_2_, f32[20,512]{1,0:T(8,128)} %get-tuple-element.64.refs_4_.refs_3_, ...), custom_call_target="tpu_custom_call" | custom-call | tf_op jit(solution)/shard_map/first_back_own_kernel/pallas_call | solution.py:1062
  84.5 0.0 all-to-all-done.3.refs_0_
  84.5 1.0 %finish_kernel.1 = (f32[3,128]{1,0:T(4,128)}, f32[3,128]{1,0:T(4,128)}) custom-call(f32[32,8,128]{2,1,0:T(8,128)S(1)} %all-to-all-done.3.refs_0_, s32[1,64]{1,0:T(1,128)S(1)} %get-tuple-element.104.refs_1_, f32[8,128]{1,0:T(8,128)S(1)} %get-tuple-element.105.refs_2_), custom_call_target="tpu_custom_call" | custom-call | tf_op jit(solution)/shard_map/finish_kernel/pallas_call | solution.py:1062
Async XLA Ops:
  2.5 16.1 %all-to-all-start = ((f32[32,1,2176]{2,1,0:T(1,128)}), f32[32,1,2176]{2,1,0:T(1,128)S(1)}, u32[]{:S(2)}, u32[]{:S(2)}) async-start(f32[32,1,2176]{2,1,0:T(1,128)} %pack_kernel.1), calls=%async_computation | async-start | bytes 557056 | tf_op jit(solution)/shard_map/all_to_all | solution.py:1088
  23.2 19.2 %all-to-all-start.1 = ((f32[32,8,512]{2,1,0:T(8,128)}), f32[32,8,512]{2,1,0:T(8,128)S(1)}, u32[]{:S(2)}, u32[]{:S(2)}) async-start(f32[32,8,512]{2,1,0:T(8,128)} %get-tuple-element.77), calls=%async_computation.1 | async-start | bytes 1048576 | tf_op jit(solution)/shard_map/all_to_all | solution.py:1088
  47.3 18.7 %all-to-all-start.2 = ((f32[32,8,512]{2,1,0:T(8,128)}), f32[32,8,512]{2,1,0:T(8,128)S(1)}, u32[]{:S(2)}, u32[]{:S(2)}) async-start(f32[32,8,512]{2,1,0:T(8,128)} %get-tuple-element.84), calls=%async_computation.2 | async-start | bytes 1048576 | tf_op jit(solution)/shard_map/all_to_all | solution.py:1088
  72.4 12.1 %all-to-all-start.3 = ((f32[32,8,128]{2,1,0:T(8,128)}), f32[32,8,128]{2,1,0:T(8,128)S(1)}, u32[]{:S(2)}, u32[]{:S(2)}) async-start(f32[32,8,128]{2,1,0:T(8,128)} %get-tuple-element.98), calls=%async_computation.3 | async-start | bytes 262144 | tf_op jit(solution)/shard_map/all_to_all | solution.py:1088
